TPU v7x, 32 devices: a whole 2x2x4 slice. The times are simulated.
32 devices in a mesh: segment: 4 (over y, x), tensor: 8 (over z, core).
Axes of the slice: x: 2, y: 2, z: 4, core: 2. Of those that a mesh axis runs over, the one named last changes fastest.
Arguments:
- hidden: bfloat16 [4, 2, 768, 3072], P('segment', None, 'tensor'), may hold values from -6 to 6
- gate_weight: bfloat16 [4, 3072, 4096], P('segment', None, 'tensor'), may hold values from -0.109375 to 0.109375
- up_weight: bfloat16 [4, 3072, 4096], P('segment', None, 'tensor'), may hold values from -0.109375 to 0.109375
- down_weight: bfloat16 [4, 4096, 3072], P('segment', 'tensor'), may hold values from -0.09375 to 0.09375
- block_rows: int32 [4, 2, 6, 128], P('segment'), may hold values from 0 to 768, as said below
- slot_gate: float32 [4, 2, 6, 128], P('segment'), may hold values from 0.1 to 1
Outputs:
- handed: bfloat16 [4, 2, 768, 3072], P('segment', None, 'tensor')
Inputs may be any that keep to these rules, and one draw needn't show every extreme that they name: `block_rows`: each entry is a token row of its micro-batch or 768 for an empty slot. Within one list of 768 slots the named rows are distinct and ascending and the empty slots come last; a list holds from 307 to 768 live slots, and both ends occur in every draw.
All inputs are finite; a program needn't handle non-finite values.
Results may differ from a plain program's by a relative error of at most 0.0085.
Values may be sent and summed in bfloat16 or wider, within the bound.
No kernel may reach another device: no remote copies, remote signals or barrier semaphores. Data moves between devices by JAX's collectives and lax.ppermute only.
A program may use at most 128 MiB of HBM per device.

v0:
```python
import functools

import jax
import jax.numpy as jnp
from jax import lax
from jax.experimental import pallas as pl
from jax.experimental.pallas import tpu as pltpu
from jax.sharding import PartitionSpec as P

CORES = 2
CHIPS = 4
BF16 = jnp.bfloat16
F32 = jnp.float32

NEAR = [(0, 1), (1, 0), (2, 3), (3, 2)]
MIDDLE = [(1, 2), (2, 1)]
OUTWARD = [(1, 0), (2, 3)]
INWARD = [(0, 1), (3, 2)]
STAY = [(0, 0), (1, 1), (2, 2), (3, 3)]


def along_line(value, pairs):
    full = [(CORES * a + c, CORES * b + c) for a, b in pairs for c in range(CORES)]
    return lax.ppermute(value, "tensor", full)


def across_cores(value):
    count = lax.axis_size("tensor")
    return lax.ppermute(value, "tensor", [(i, i ^ 1) for i in range(count)])


def to_next_phase(value, pairs, cross):
    segments, count = lax.axis_size("segment"), lax.axis_size("tensor")
    full = [
        (s * count + CORES * a + c, ((s + 1) % segments) * count + CORES * b + (c ^ cross))
        for s in range(segments)
        for a, b in pairs
        for c in range(CORES)
    ]
    return lax.ppermute(value, ("segment", "tensor"), full)


def ffn_kernel(layout, *refs):
    n_in = sum(choices for _, choices in layout)
    n_out = len(layout)
    meta, slot_rows, slot_gates = refs[:3]
    x_refs = refs[3 : 3 + n_in]
    weights = refs[3 + n_in : 9 + n_in]
    outs = refs[9 + n_in : 9 + n_in + n_out]
    x, h, gate, wg, wu, wd, sem_g, sem_u, sem_d = refs[9 + n_in + n_out :]
    tiles, _, width = wg.shape
    columns, _, out_width = wd.shape
    per_core = tiles // CORES
    deep = per_core * width

    copies_in, copies_out = [], []
    for tile in range(tiles):
        core, part = tile // per_core, tile % per_core
        span = pl.ds(part * width, width)
        g = pltpu.make_async_copy(weights[3 * core].at[:, span], wg.at[tile], sem_g.at[tile])
        u = pltpu.make_async_copy(weights[3 * core + 1].at[:, span], wu.at[tile], sem_u.at[tile])
        g.start()
        u.start()
        copies_in.append((g, u))
    for column in range(columns):
        pair = []
        for core in range(CORES):
            d = pltpu.make_async_copy(
                weights[3 * core + 2].at[:, pl.ds(column * out_width, out_width)],
                wd.at[column, pl.ds(core * deep, deep)],
                sem_d.at[column, core],
            )
            d.start()
            pair.append(d)
        copies_out.append(pair)

    second = meta[0] == 1
    start, at = 0, 0
    for block, (rows, choices) in enumerate(layout):
        here = pl.ds(start, rows)
        if choices == 1:
            x[here, :] = x_refs[at][...]
        else:
            first_ref, second_ref = x_refs[at], x_refs[at + 1]

            @pl.when(second)
            def _(here=here, ref=second_ref):
                x[here, :] = ref[...]

            @pl.when(jnp.logical_not(second))
            def _(here=here, ref=first_ref):
                x[here, :] = ref[...]

        half_rows = rows // CORES
        for half in range(CORES):
            tokens = meta[1 + CORES * block + half] + lax.broadcasted_iota(
                jnp.int32, (half_rows, slot_rows.shape[1]), 0
            )
            named = jnp.where(slot_rows[...] == tokens, slot_gates[...], 0.0)
            column = jnp.sum(named, axis=1, keepdims=True)
            gate[pl.ds(start + half * half_rows, half_rows), :] = jnp.broadcast_to(
                column, (half_rows, gate.shape[1])
            )
        start += rows
        at += choices

    for tile in range(tiles):
        for copy in copies_in[tile]:
            copy.wait()
        g = jnp.dot(x[...], wg[tile], preferred_element_type=F32)
        u = jnp.dot(x[...], wu[tile], preferred_element_type=F32)
        h[:, tile * width : (tile + 1) * width] = (g / (1.0 + jnp.exp(-g)) * u).astype(BF16)
    for column in range(columns):
        for copy in copies_out[column]:
            copy.wait()
        span = slice(column * out_width, (column + 1) * out_width)
        y = jnp.dot(h[...], wd[column], preferred_element_type=F32)
        y = (y * gate[:, :1]).astype(BF16)
        start = 0
        for (rows, _), out in zip(layout, outs):
            out[:, span] = y[start : start + rows, :]
            start += rows


def ffn(meta, slot_rows, slot_gates, blocks, weights):
    layout = tuple((block[0].shape[0], len(block)) for block in blocks)
    features, hidden_units = weights[0].shape
    total = sum(rows for rows, _ in layout)
    width = 256 if hidden_units % 256 == 0 else hidden_units
    tiles = CORES * hidden_units // width
    out_width = 768 if features % 768 == 0 else features
    columns = features // out_width
    any_space = pl.BlockSpec(memory_space=pl.ANY)
    vmem = pl.BlockSpec(memory_space=pltpu.VMEM)
    flat = [choice for block in blocks for choice in block]
    return pl.pallas_call(
        functools.partial(ffn_kernel, layout),
        out_shape=[jax.ShapeDtypeStruct((rows, features), BF16) for rows, _ in layout],
        in_specs=[pl.BlockSpec(memory_space=pltpu.SMEM), vmem, vmem]
        + [vmem] * len(flat)
        + [any_space] * 6,
        out_specs=[vmem] * len(layout),
        scratch_shapes=[
            pltpu.VMEM((total, features), BF16),
            pltpu.VMEM((total, CORES * hidden_units), BF16),
            pltpu.VMEM((total, 128), F32),
            pltpu.VMEM((tiles, features, width), BF16),
            pltpu.VMEM((tiles, features, width), BF16),
            pltpu.VMEM((columns, CORES * hidden_units, out_width), BF16),
            pltpu.SemaphoreType.DMA((tiles,)),
            pltpu.SemaphoreType.DMA((tiles,)),
            pltpu.SemaphoreType.DMA((columns, CORES)),
        ],
        compiler_params=pltpu.CompilerParams(vmem_limit_bytes=44 * 1024 * 1024),
        cost_estimate=pl.CostEstimate(
            flops=12 * total * features * hidden_units,
            bytes_accessed=12 * features * hidden_units,
            transcendentals=total * CORES * hidden_units,
        ),
    )(meta, slot_rows, slot_gates, *flat, *weights)


def add(*values):
    return sum(value.astype(F32) for value in values).astype(BF16)


def staged(hidden, gate_weight, up_weight, down_weight, block_rows, slot_gate, chunks):
    rows_here, features = hidden.shape[2], hidden.shape[3]
    slots = block_rows.shape[2] * block_rows.shape[3]
    index = lax.axis_index("tensor")
    core, chip = index % CORES, index // CORES
    right = chip >= CHIPS // 2
    inner = jnp.logical_and(chip > 0, chip < CHIPS - 1)

    mine = lax.dynamic_index_in_dim(hidden[0], core, 0, keepdims=False)
    theirs = lax.dynamic_index_in_dim(hidden[0], 1 - core, 0, keepdims=False)
    slot_rows = lax.dynamic_index_in_dim(block_rows[0], core, 0, keepdims=False).reshape(1, slots)
    slot_gates = lax.dynamic_index_in_dim(slot_gate[0], core, 0, keepdims=False).reshape(1, slots)

    other = across_cores(theirs)
    other, *own_weights = lax.optimization_barrier(
        (other, gate_weight[0], up_weight[0], down_weight[0])
    )
    weights = own_weights + [across_cores(weight) for weight in own_weights]

    spans, start = [], 0
    for size in chunks:
        spans.append((start, size))
        start += size

    def token(mirrored_block, half, offset):
        block = jnp.where(right, CHIPS - 1 - mirrored_block, mirrored_block)
        owner = block * CORES + jnp.where(half == 0, core, 1 - core)
        return owner * rows_here + offset

    def meta_of(blocks, flag):
        values = [flag.astype(jnp.int32)]
        for mirrored_block, offset in blocks:
            values += [token(mirrored_block, half, offset) for half in range(CORES)]
        return jnp.stack(values).astype(jnp.int32)

    own_block = inner.astype(jnp.int32)
    near_block = 1 - own_block

    own = jnp.concatenate([mine, other], axis=0)
    pieces = [
        jnp.concatenate([mine[o : o + n], other[o : o + n]], axis=0) for o, n in spans
    ]

    near = along_line(own, NEAR)
    second_at_inner = [along_line(piece, MIDDLE) for piece in pieces]
    second_at_outer = [along_line(piece, OUTWARD) for piece in second_at_inner]
    near_pieces = [
        jnp.concatenate(
            [near[o : o + n], near[rows_here + o : rows_here + o + n]], axis=0
        )
        for o, n in spans
    ]
    third_at_inner = [along_line(piece, MIDDLE) for piece in near_pieces]
    third_at_outer = [along_line(piece, OUTWARD) for piece in third_at_inner]

    own_part, near_part = ffn(
        meta_of([(own_block, 0), (near_block, 0)], jnp.int32(0)),
        slot_rows,
        slot_gates,
        [(own,), (near,)],
        weights,
    )
    from_end = along_line(near_part, INWARD)

    base = add(own, own_part, from_end)
    base_same = to_next_phase(base[:rows_here], STAY, 0)
    base_cross = to_next_phase(base[rows_here:], STAY, 1)

    same, cross = [], []
    for (o, n), a2, b2, a3, b3 in zip(
        spans, second_at_outer, second_at_inner, third_at_outer, third_at_inner
    ):
        part2, part3 = ffn(
            meta_of([(2, o), (3, o)], inner),
            slot_rows,
            slot_gates,
            [(a2, b2), (a3, b3)],
            weights,
        )
        sum3 = add(part3, along_line(part3, INWARD))
        sum2 = add(part2, along_line(part2, INWARD))
        over = along_line(sum3, MIDDLE)
        for_end = add(
            jnp.concatenate(
                [near_part[o : o + n], near_part[rows_here + o : rows_here + o + n]], axis=0
            ),
            over,
        )
        got_same = [base_same[o : o + n]]
        got_cross = [base_cross[o : o + n]]
        for value, pairs in ((sum2, MIDDLE), (for_end, OUTWARD)):
            got_same.append(to_next_phase(value[:n], pairs, 0))
            got_cross.append(to_next_phase(value[n:], pairs, 1))
        same.append(add(*got_same))
        cross.append(add(*got_cross))
    same = jnp.concatenate(same, axis=0)
    cross = jnp.concatenate(cross, axis=0)
    low = core == 0
    return jnp.stack([jnp.where(low, same, cross), jnp.where(low, cross, same)])[None]


def whole_gather(hidden, gate_weight, up_weight, down_weight, block_rows, slot_gate):
    rows_here = hidden.shape[2]
    slots = block_rows.shape[2] * block_rows.shape[3]
    total_rows = rows_here * lax.axis_size("tensor")
    gathered = lax.all_gather(hidden, "tensor", axis=2, tiled=True)
    results = []
    for micro_batch in range(hidden.shape[1]):
        x = gathered[0, micro_batch]
        slot_rows = block_rows[0, micro_batch].reshape(1, slots)
        slot_gates = slot_gate[0, micro_batch].reshape(1, slots)
        tokens = lax.broadcasted_iota(jnp.int32, (total_rows, 1), 0)
        gate = jnp.sum(jnp.where(slot_rows == tokens, slot_gates, 0.0), axis=1, keepdims=True)
        gate_act = jnp.dot(x, gate_weight[0], preferred_element_type=F32)
        up_act = jnp.dot(x, up_weight[0], preferred_element_type=F32)
        hidden_act = (jax.nn.silu(gate_act) * up_act).astype(BF16)
        part = jnp.dot(hidden_act, down_weight[0], preferred_element_type=F32) * gate
        placed = lax.psum_scatter(
            part.astype(BF16), "tensor", scatter_dimension=0, tiled=True
        )
        results.append(add(hidden[0, micro_batch], placed))
    count = lax.axis_size("segment")
    pairs = [(source, (source + 1) % count) for source in range(count)]
    return lax.ppermute(jnp.stack(results)[None], "segment", pairs)


def per_device(*args):
    rows_here = args[0].shape[2]
    if (
        lax.axis_size("tensor") != CORES * CHIPS
        or args[0].shape[1] != CORES
        or rows_here % 32 != 0
    ):
        return whole_gather(*args)
    return staged(*args, chunks=CHUNKS(rows_here))


def CHUNKS(rows):
    return [rows // 2, rows // 2]


def solution(mesh):
    return jax.shard_map(
        per_device,
        mesh=mesh,
        in_specs=(
            P("segment", None, "tensor", None),
            P("segment", None, "tensor"),
            P("segment", None, "tensor"),
            P("segment", "tensor", None),
            P("segment", None, None, None),
            P("segment", None, None, None),
        ),
        out_specs=P("segment", None, "tensor", None),
        check_vma=False,
    )
```

profile of v0, /device:TPU:0, one launch (start us, length us, event | category | flops | bytes accessed | tf_op | source)
XLA Modules:
  0.0 235.1 jit_solution(10532281635510452711)
XLA Ops:
  0.0 2.2 dynamic-slice_bitcast_fusion.1
  2.2 0.5 collective-permute-start
  2.7 1.6 collective-permute-done
  4.3 0.8 copy-done.12
  5.1 1.4 pad_maximum_fusion.refs_3_
  6.5 3.0 %collective-permute-start.1 = (bf16[192,3072]{1,0:T(8,128)(2,1)S(1)}, bf16[192,3072]{1,0:T(8,128)(2,1)S(1)}, u32[]{:S(2)}, u32[]{:S(2)}) collective-permute-start(bf16[192,3072]{1,0:T(8,128)(2,1)S(1)} %pad_maximum_fusion.refs_3_), channel_id=1, source_target_pairs={{0,2},{1,3},{2,0},{3,1},{4,6},{5,7},{6,4},{7,5},{8,10},{9,11},{10,... | collective-permute-start | bytes 3538952 | tf_op jit(solution)/shard_map/ppermute | solution.py:24
  9.5 1.1 fusion.11
  10.7 0.5 collective-permute-start.3
  11.4 0.7 collective-permute-start.16
  12.1 1.5 collective-permute-start.7
  13.7 22.2 %collective-permute-done.1.refs_4_ = bf16[192,3072]{1,0:T(8,128)(2,1)S(1)} collective-permute-done((bf16[192,3072]{1,0:T(8,128)(2,1)S(1)}, bf16[192,3072]{1,0:T(8,128)(2,1)S(1)}, u32[]{:S(2)}, u32[]{:S(2)}) %collective-permute-start.1) | collective-permute-done | bytes 1179680 | tf_op jit(solution)/shard_map/ppermute | solution.py:24
  35.8 1.3 collective-permute-start.17
  37.3 1.5 collective-permute-start.18
  38.8 0.9 pad_maximum_fusion.2
  39.7 12.9 %collective-permute-done.17.refs_3_ = bf16[96,3072]{1,0:T(8,128)(2,1)S(1)} collective-permute-done((bf16[96,3072]{1,0:T(8,128)(2,1)S(1)}, bf16[96,3072]{1,0:T(8,128)(2,1)S(1)}, u32[]{:S(2)}, u32[]{:S(2)}) %collective-permute-start.17) | collective-permute-done | bytes 589856 | tf_op jit(solution)/shard_map/ppermute | solution.py:24
  52.6 0.8 copy-done.10
  53.4 1.5 collective-permute-start.9
  54.9 1.3 collective-permute-start.19
  56.5 1.3 collective-permute-start.8
  57.8 18.9 %collective-permute-done.19.refs_5_ = bf16[96,3072]{1,0:T(8,128)(2,1)} collective-permute-done((bf16[96,3072]{1,0:T(8,128)(2,1)}, bf16[96,3072]{1,0:T(8,128)(2,1)}, u32[]{:S(2)}, u32[]{:S(2)}) %collective-permute-start.19) | collective-permute-done | bytes 589856 | tf_op jit(solution)/shard_map/ppermute | solution.py:24
  76.7 1.3 collective-permute-start.10
  78.1 1.9 copy-done.2
  80.0 1.1 copy-done.9
  81.0 1.1 copy-done.11
  82.1 9.6 %shard_map.66 = (bf16[96,3072]{1,0:T(8,128)(2,1)S(1)}, bf16[96,3072]{1,0:T(8,128)(2,1)S(1)}) custom-call(s32[5]{0:T(128)S(1)} %stack.69.refs_0_, s32[1,768]{1,0:T(1,128)S(1)} %dynamic-slice_bitcast_fusion.5.refs_1_, f32[1,768]{1,0:T(1,128)S(1)} %dynamic-slice_bitcast_fusion.4.refs_2_, bf16[96,3072]{1,0:T(8,128)(2,1)S(1)} %copy-done.11, ...), custom_call_target="tpu_custom_call" | custom-call | flops 3623878656 | bytes 18874368 | tf_op jit(solution)/shard_map/pallas_call | solution.py:136
  91.6 4.8 %collective-permute-start.20 = (bf16[96,3072]{1,0:T(8,128)(2,1)S(1)}, bf16[96,3072]{1,0:T(8,128)(2,1)S(1)}, u32[]{:S(2)}, u32[]{:S(2)}) collective-permute-start(bf16[96,3072]{1,0:T(8,128)(2,1)S(1)} %get-tuple-element.23), channel_id=1, source_target_pairs={{0,2},{1,3},{6,4},{7,5},{8,10},{9,11},{14,12},{15,13},{16,18},{17,... | collective-permute-start | bytes 1769480 | tf_op jit(solution)/shard_map/ppermute | solution.py:24
  96.5 12.3 %shard_map.64 = (bf16[192,3072]{1,0:T(8,128)(2,1)S(1)}, bf16[192,3072]{1,0:T(8,128)(2,1)S(1)}) custom-call(s32[5]{0:T(128)S(1)} %stack.58.refs_0_, s32[1,768]{1,0:T(1,128)S(1)} %dynamic-slice_bitcast_fusion.5.refs_1_, f32[1,768]{1,0:T(1,128)S(1)} %dynamic-slice_bitcast_fusion.4.refs_2_, bf16[192,3072]{1,0:T(8,128)(2,1)S(1)} %copy-done.5, ...), custom_call_target="tpu_custom_call" | custom-call | flops 7247757312 | bytes 18874368 | tf_op jit(solution)/shard_map/pallas_call | solution.py:136
  108.7 1.4 collective-permute-start.5
  110.1 9.4 %shard_map.65 = (bf16[96,3072]{1,0:T(8,128)(2,1)S(1)}, bf16[96,3072]{1,0:T(8,128)(2,1)S(1)}) custom-call(s32[5]{0:T(128)S(1)} %stack.64.refs_0_, s32[1,768]{1,0:T(1,128)S(1)} %dynamic-slice_bitcast_fusion.5.refs_1_, f32[1,768]{1,0:T(1,128)S(1)} %dynamic-slice_bitcast_fusion.4.refs_2_, bf16[96,3072]{1,0:T(8,128)(2,1)S(1)} %collective-permute-done.8.refs_3_, ...), custom_call_target="tpu_custom_call" | custom-call | flops 3623878656 | bytes 18874368 | tf_op jit(solution)/shard_map/pallas_call | solution.py:136
  119.6 1.3 collective-permute-start.11
  120.9 1.3 collective-permute-start.13
  122.2 1.5 collective-permute-start.22
  123.9 0.1 add_convert_fusion.3
  124.0 0.7 fusion.9
  124.8 0.7 collective-permute-start.21
  125.5 36.3 %collective-permute-done.13 = bf16[96,3072]{1,0:T(8,128)(2,1)S(1)} collective-permute-done((bf16[96,3072]{1,0:T(8,128)(2,1)S(1)}, bf16[96,3072]{1,0:T(8,128)(2,1)S(1)}, u32[]{:S(2)}, u32[]{:S(2)}) %collective-permute-start.13) | collective-permute-done | bytes 589856 | tf_op jit(solution)/shard_map/ppermute | solution.py:24
  161.7 0.1 add_convert_fusion.5
  161.9 0.7 collective-permute-start.14
  162.6 7.0 %collective-permute-done.22 = bf16[96,3072]{1,0:T(8,128)(2,1)S(1)} collective-permute-done((bf16[96,3072]{1,0:T(8,128)(2,1)S(1)}, bf16[96,3072]{1,0:T(8,128)(2,1)S(1)}, u32[]{:S(2)}, u32[]{:S(2)}) %collective-permute-start.22) | collective-permute-done | bytes 589856 | tf_op jit(solution)/shard_map/ppermute | solution.py:24
  169.6 0.1 add_convert_fusion.2
  169.8 0.7 collective-permute-start.23
  170.5 0.1 add_convert_fusion.6
  170.6 0.8 fusion.7
  171.4 0.7 collective-permute-start.12
  172.1 0.4 add_convert_fusion.1
  172.5 0.9 fusion.8
  173.4 1.3 collective-permute-start.15
  174.7 0.6 add_convert_fusion
  175.4 1.5 collective-permute-start.6
  176.9 0.8 fusion.10
  177.8 1.3 collective-permute-start.24
  179.1 0.7 collective-permute-start.28
  179.8 0.7 collective-permute-start.26
  180.5 20.8 %collective-permute-done.15 = bf16[48,3072]{1,0:T(8,128)(2,1)S(1)} collective-permute-done((bf16[48,3072]{1,0:T(8,128)(2,1)}, bf16[48,3072]{1,0:T(8,128)(2,1)S(1)}, u32[]{:S(2)}, u32[]{:S(2)}) %collective-permute-start.15) | collective-permute-done | bytes 294944 | tf_op jit(solution)/shard_map/ppermute | solution.py:40
  201.3 1.3 collective-permute-start.27
  202.6 2.1 collective-permute-done.24
  204.7 1.3 collective-permute-start.29
  206.0 0.2 fusion
  206.3 6.2 %collective-permute-done.27 = bf16[48,3072]{1,0:T(8,128)(2,1)S(1)} collective-permute-done((bf16[48,3072]{1,0:T(8,128)(2,1)}, bf16[48,3072]{1,0:T(8,128)(2,1)S(1)}, u32[]{:S(2)}, u32[]{:S(2)}) %collective-permute-start.27) | collective-permute-done | bytes 294944 | tf_op jit(solution)/shard_map/ppermute | solution.py:40
  212.5 6.3 %collective-permute-done.29 = bf16[48,3072]{1,0:T(8,128)(2,1)S(1)} collective-permute-done((bf16[48,3072]{1,0:T(8,128)(2,1)}, bf16[48,3072]{1,0:T(8,128)(2,1)S(1)}, u32[]{:S(2)}, u32[]{:S(2)}) %collective-permute-start.29) | collective-permute-done | bytes 294944 | tf_op jit(solution)/shard_map/ppermute | solution.py:40
  218.8 14.7 %collective-permute-done.25 = bf16[96,3072]{1,0:T(8,128)(2,1)S(1)} collective-permute-done((bf16[96,3072]{1,0:T(8,128)(2,1)S(1)}, bf16[96,3072]{1,0:T(8,128)(2,1)S(1)}, u32[]{:S(2)}, u32[]{:S(2)}) %collective-permute-start.25) | collective-permute-done | bytes 589856 | tf_op jit(solution)/shard_map/ppermute | solution.py:40
  233.5 0.2 fusion.2
  233.7 0.2 broadcast_select_fusion.1
  233.9 1.1 maximum_bitcast_fusion
  (65 shorter events, 1.0 us)
Async XLA Ops:
  0.0 56.5 %copy-start = (f32[1,2,6,128]{3,1,2,0:T(2,128)S(1)}, f32[1,2,6,128]{3,1,2,0:T(2,128)}, u32[]{:S(2)}) copy-start(f32[1,2,6,128]{3,1,2,0:T(2,128)} %param.11) | copy-start | bytes 18436
  0.0 2.7 %copy-start.16 = (bf16[1,2,96,3072]{3,2,1,0:T(8,128)(2,1)S(1)}, bf16[1,2,96,3072]{3,2,1,0:T(8,128)(2,1)}, u32[]{:S(2)}) copy-start(bf16[1,2,96,3072]{3,2,1,0:T(8,128)(2,1)} %param.6) | copy-start | bytes 3538948
  2.2 2.1 collective-permute-start
  2.7 2.5 %copy-start.14 = (bf16[96,3072]{1,0:T(8,128)(2,1)S(1)}, bf16[96,3072]{1,0:T(8,128)(2,1)}, u32[]{:S(2)}) copy-start(bf16[96,3072]{1,0:T(8,128)(2,1)} %get-tuple-element.39) | copy-start | bytes 1769476
  4.3 0.8 copy-start.12
  5.1 5.5 %copy-start.1 = (bf16[1,3072,512]{2,1,0:T(8,128)(2,1)S(1)}, bf16[1,3072,512]{2,1,0:T(8,128)(2,1)}, u32[]{:S(2)}) copy-start(bf16[1,3072,512]{2,1,0:T(8,128)(2,1)} %param.7) | copy-start | bytes 9437188
  6.5 4.8 %copy-start.4 = (bf16[192,3072]{1,0:T(8,128)(2,1)}, bf16[192,3072]{1,0:T(8,128)(2,1)S(1)}, u32[]{:S(2)}) copy-start(bf16[192,3072]{1,0:T(8,128)(2,1)S(1)} %pad_maximum_fusion.refs_3_) | copy-start | bytes 3538948
  6.5 29.3 %collective-permute-start.1 = (bf16[192,3072]{1,0:T(8,128)(2,1)S(1)}, bf16[192,3072]{1,0:T(8,128)(2,1)S(1)}, u32[]{:S(2)}, u32[]{:S(2)}) collective-permute-start(bf16[192,3072]{1,0:T(8,128)(2,1)S(1)} %pad_maximum_fusion.refs_3_), channel_id=1, source_target_pairs={{0,2},{1,3},{2,0},{3,1},{4,6},{5,7},{6,4},{7,5},{8,10},{9,11},{10,... | collective-permute-start | bytes 3538952 | tf_op jit(solution)/shard_map/ppermute | solution.py:24
  10.6 67.4 %collective-permute-start.2 = (bf16[3072,512]{1,0:T(8,128)(2,1)S(1)}, bf16[3072,512]{1,0:T(8,128)(2,1)}, u32[]{:S(2)}, u32[]{:S(2)}) collective-permute-start(bf16[3072,512]{1,0:T(8,128)(2,1)S(1)} %bitcast.38), channel_id=1, source_target_pairs={{0,1},{1,0},{2,3},{3,2},{4,5},{5,4},{6,7},{7,6},{8,9},{9,8},{10,11... | collective-permute-start | bytes 9437192 | tf_op jit(solution)/shard_map/ppermute | solution.py:29
  10.7 67.3 %collective-permute-start.3 = (bf16[3072,512]{1,0:T(8,128)(2,1)}, bf16[3072,512]{1,0:T(8,128)(2,1)}, u32[]{:S(2)}, u32[]{:S(2)}) collective-permute-start(bf16[3072,512]{1,0:T(8,128)(2,1)} %bitcast.42), channel_id=1, source_target_pairs={{0,1},{1,0},{2,3},{3,2},{4,5},{5,4},{6,7},{7,6},{8,9},{9,8},{10,11... | collective-permute-start | bytes 9437192 | tf_op jit(solution)/shard_map/ppermute | solution.py:29
  11.2 66.8 %collective-permute-start.4 = (bf16[512,3072]{1,0:T(8,128)(2,1)}, bf16[512,3072]{1,0:T(8,128)(2,1)}, u32[]{:S(2)}, u32[]{:S(2)}) collective-permute-start(bf16[512,3072]{1,0:T(8,128)(2,1)} %bitcast.46), channel_id=1, source_target_pairs={{0,1},{1,0},{2,3},{3,2},{4,5},{5,4},{6,7},{7,6},{8,9},{9,8},{10,11... | collective-permute-start | bytes 9437192 | tf_op jit(solution)/shard_map/ppermute | solution.py:29
  11.4 0.8 collective-permute-start.16
  12.1 25.1 %copy-start.8 = (bf16[96,3072]{1,0:T(8,128)(2,1)}, bf16[96,3072]{1,0:T(8,128)(2,1)S(1)}, u32[]{:S(2)}) copy-start(bf16[96,3072]{1,0:T(8,128)(2,1)S(1)} %collective-permute-done.16.refs_4_) | copy-start | bytes 1769476
  12.1 25.1 %collective-permute-start.7 = (bf16[96,3072]{1,0:T(8,128)(2,1)S(1)}, bf16[96,3072]{1,0:T(8,128)(2,1)}, u32[]{:S(2)}, u32[]{:S(2)}) collective-permute-start(bf16[96,3072]{1,0:T(8,128)(2,1)S(1)} %pad_maximum_fusion.1), channel_id=1, source_target_pairs={{2,4},{3,5},{4,2},{5,3},{10,12},{11,13},{12,10},{13,11},{18,20},{1... | collective-permute-start | bytes 1769480 | tf_op jit(solution)/shard_map/ppermute | solution.py:24
  35.8 1.4 copy-start.6
  35.8 16.7 %collective-permute-start.17 = (bf16[96,3072]{1,0:T(8,128)(2,1)S(1)}, bf16[96,3072]{1,0:T(8,128)(2,1)S(1)}, u32[]{:S(2)}, u32[]{:S(2)}) collective-permute-start(bf16[96,3072]{1,0:T(8,128)(2,1)S(1)} %collective-permute-done.16.refs_4_), channel_id=1, source_target_pairs={{2,0},{3,1},{4,6},{5,7},{10,8},{11,9},{12,14},{13,15},{18,16},{19,... | collective-permute-start | bytes 1769480 | tf_op jit(solution)/shard_map/ppermute | solution.py:24
  37.2 19.3 %copy-start.17 = (s32[1,2,6,128]{3,1,2,0:T(2,128)S(1)}, s32[1,2,6,128]{3,1,2,0:T(2,128)}, u32[]{:S(2)}) copy-start(s32[1,2,6,128]{3,1,2,0:T(2,128)} %param.10) | copy-start | bytes 18436
  37.3 17.6 %collective-permute-start.18 = (bf16[96,3072]{1,0:T(8,128)(2,1)S(1)}, bf16[96,3072]{1,0:T(8,128)(2,1)}, u32[]{:S(2)}, u32[]{:S(2)}) collective-permute-start(bf16[96,3072]{1,0:T(8,128)(2,1)S(1)} %pad_maximum_fusion.4), channel_id=1, source_target_pairs={{2,4},{3,5},{4,2},{5,3},{10,12},{11,13},{12,10},{13,11},{18,20},{1... | collective-permute-start | bytes 1769480 | tf_op jit(solution)/shard_map/ppermute | solution.py:24
  52.6 0.8 copy-start.10
  53.4 3.1 %collective-permute-start.9 = (bf16[96,3072]{1,0:T(8,128)(2,1)}, bf16[96,3072]{1,0:T(8,128)(2,1)}, u32[]{:S(2)}, u32[]{:S(2)}) collective-permute-start(bf16[96,3072]{1,0:T(8,128)(2,1)} %pad_maximum_fusion.2), channel_id=1, source_target_pairs={{2,4},{3,5},{4,2},{5,3},{10,12},{11,13},{12,10},{13,11},{18,20},{1... | collective-permute-start | bytes 1769480 | tf_op jit(solution)/shard_map/ppermute | solution.py:24
  54.9 21.9 %collective-permute-start.19 = (bf16[96,3072]{1,0:T(8,128)(2,1)}, bf16[96,3072]{1,0:T(8,128)(2,1)}, u32[]{:S(2)}, u32[]{:S(2)}) collective-permute-start(bf16[96,3072]{1,0:T(8,128)(2,1)} %collective-permute-done.18.refs_6_), channel_id=1, source_target_pairs={{2,0},{3,1},{4,6},{5,7},{10,8},{11,9},{12,14},{13,15},{18,16},{19,... | collective-permute-start | bytes 1769480 | tf_op jit(solution)/shard_map/ppermute | solution.py:24
  56.5 53.6 %collective-permute-start.8 = (bf16[96,3072]{1,0:T(8,128)(2,1)}, bf16[96,3072]{1,0:T(8,128)(2,1)S(1)}, u32[]{:S(2)}, u32[]{:S(2)}) collective-permute-start(bf16[96,3072]{1,0:T(8,128)(2,1)} %collective-permute-done.7.refs_4_), channel_id=1, source_target_pairs={{2,0},{3,1},{4,6},{5,7},{10,8},{11,9},{12,14},{13,15},{18,16},{19,... | collective-permute-start | bytes 1769480 | tf_op jit(solution)/shard_map/ppermute | solution.py:24
  76.7 33.4 %collective-permute-start.10 = (bf16[96,3072]{1,0:T(8,128)(2,1)}, bf16[96,3072]{1,0:T(8,128)(2,1)S(1)}, u32[]{:S(2)}, u32[]{:S(2)}) collective-permute-start(bf16[96,3072]{1,0:T(8,128)(2,1)} %collective-permute-done.9.refs_6_), channel_id=1, source_target_pairs={{2,0},{3,1},{4,6},{5,7},{10,8},{11,9},{12,14},{13,15},{18,16},{19,... | collective-permute-start | bytes 1769480 | tf_op jit(solution)/shard_map/ppermute | solution.py:24
  78.1 1.9 copy-start.2
  80.0 1.1 copy-start.9
  81.0 1.1 copy-start.11
  82.1 14.4 %copy-start.5 = (bf16[192,3072]{1,0:T(8,128)(2,1)S(1)}, bf16[192,3072]{1,0:T(8,128)(2,1)}, u32[]{:S(2)}) copy-start(bf16[192,3072]{1,0:T(8,128)(2,1)} %copy-done.4) | copy-start | bytes 3538948
  82.1 14.4 %copy-start.7 = (bf16[192,3072]{1,0:T(8,128)(2,1)S(1)}, bf16[192,3072]{1,0:T(8,128)(2,1)}, u32[]{:S(2)}) copy-start(bf16[192,3072]{1,0:T(8,128)(2,1)} %copy-done.6) | copy-start | bytes 3538948
  91.6 32.2 %collective-permute-start.20 = (bf16[96,3072]{1,0:T(8,128)(2,1)S(1)}, bf16[96,3072]{1,0:T(8,128)(2,1)S(1)}, u32[]{:S(2)}, u32[]{:S(2)}) collective-permute-start(bf16[96,3072]{1,0:T(8,128)(2,1)S(1)} %get-tuple-element.23), channel_id=1, source_target_pairs={{0,2},{1,3},{6,4},{7,5},{8,10},{9,11},{14,12},{15,13},{16,18},{17,... | collective-permute-start | bytes 1769480 | tf_op jit(solution)/shard_map/ppermute | solution.py:24
  96.5 13.7 %copy-start.3 = (bf16[1,3072,512]{2,1,0:T(8,128)(2,1)S(1)}, bf16[1,3072,512]{2,1,0:T(8,128)(2,1)}, u32[]{:S(2)}) copy-start(bf16[1,3072,512]{2,1,0:T(8,128)(2,1)} %param.8) | copy-start | bytes 9437188
  108.7 65.9 %collective-permute-start.5 = (bf16[192,3072]{1,0:T(8,128)(2,1)S(1)}, bf16[192,3072]{1,0:T(8,128)(2,1)S(1)}, u32[]{:S(2)}, u32[]{:S(2)}) collective-permute-start(bf16[192,3072]{1,0:T(8,128)(2,1)S(1)} %get-tuple-element.20), channel_id=1, source_target_pairs={{0,2},{1,3},{6,4},{7,5},{8,10},{9,11},{14,12},{15,13},{16,18},{17,... | collective-permute-start | bytes 3538952 | tf_op jit(solution)/shard_map/ppermute | solution.py:24
  119.6 50.9 %collective-permute-start.11 = (bf16[96,3072]{1,0:T(8,128)(2,1)S(1)}, bf16[96,3072]{1,0:T(8,128)(2,1)S(1)}, u32[]{:S(2)}, u32[]{:S(2)}) collective-permute-start(bf16[96,3072]{1,0:T(8,128)(2,1)S(1)} %get-tuple-element.21), channel_id=1, source_target_pairs={{0,2},{1,3},{6,4},{7,5},{8,10},{9,11},{14,12},{15,13},{16,18},{17,... | collective-permute-start | bytes 1769480 | tf_op jit(solution)/shard_map/ppermute | solution.py:24
  120.9 40.8 %collective-permute-start.13 = (bf16[96,3072]{1,0:T(8,128)(2,1)S(1)}, bf16[96,3072]{1,0:T(8,128)(2,1)S(1)}, u32[]{:S(2)}, u32[]{:S(2)}) collective-permute-start(bf16[96,3072]{1,0:T(8,128)(2,1)S(1)} %get-tuple-element.22), channel_id=1, source_target_pairs={{0,2},{1,3},{6,4},{7,5},{8,10},{9,11},{14,12},{15,13},{16,18},{17,... | collective-permute-start | bytes 1769480 | tf_op jit(solution)/shard_map/ppermute | solution.py:24
  122.2 47.4 %collective-permute-start.22 = (bf16[96,3072]{1,0:T(8,128)(2,1)S(1)}, bf16[96,3072]{1,0:T(8,128)(2,1)S(1)}, u32[]{:S(2)}, u32[]{:S(2)}) collective-permute-start(bf16[96,3072]{1,0:T(8,128)(2,1)S(1)} %get-tuple-element.24), channel_id=1, source_target_pairs={{0,2},{1,3},{6,4},{7,5},{8,10},{9,11},{14,12},{15,13},{16,18},{17,... | collective-permute-start | bytes 1769480 | tf_op jit(solution)/shard_map/ppermute | solution.py:24
  124.8 54.3 %collective-permute-start.21 = (bf16[48,3072]{1,0:T(8,128)(2,1)}, bf16[48,3072]{1,0:T(8,128)(2,1)S(1)}, u32[]{:S(2)}, u32[]{:S(2)}) collective-permute-start(bf16[48,3072]{1,0:T(8,128)(2,1)} %get-tuple-element.47), channel_id=1, source_target_pairs={{2,12},{3,13},{4,10},{5,11},{10,20},{11,21},{12,18},{13,19},{18,28... | collective-permute-start | bytes 884744 | tf_op jit(solution)/shard_map/ppermute | solution.py:40
  161.9 10.2 %collective-permute-start.14 = (bf16[96,3072]{1,0:T(8,128)(2,1)S(1)}, bf16[96,3072]{1,0:T(8,128)(2,1)S(1)}, u32[]{:S(2)}, u32[]{:S(2)}) collective-permute-start(bf16[96,3072]{1,0:T(8,128)(2,1)S(1)} %add_convert_fusion.5), channel_id=1, source_target_pairs={{2,4},{3,5},{4,2},{5,3},{10,12},{11,13},{12,10},{13,11},{18,20},{1... | collective-permute-start | bytes 1769480 | tf_op jit(solution)/shard_map/ppermute | solution.py:24
  169.8 2.3 collective-permute-start.23
  171.4 8.4 %collective-permute-start.12 = (bf16[48,3072]{1,0:T(8,128)(2,1)}, bf16[48,3072]{1,0:T(8,128)(2,1)S(1)}, u32[]{:S(2)}, u32[]{:S(2)}) collective-permute-start(bf16[48,3072]{1,0:T(8,128)(2,1)} %get-tuple-element.43), channel_id=1, source_target_pairs={{2,12},{3,13},{4,10},{5,11},{10,20},{11,21},{12,18},{13,19},{18,28... | collective-permute-start | bytes 884744 | tf_op jit(solution)/shard_map/ppermute | solution.py:40
  172.5 2.2 copy-start.13
  172.5 2.2 copy-start.15
  173.4 27.9 %collective-permute-start.15 = (bf16[48,3072]{1,0:T(8,128)(2,1)}, bf16[48,3072]{1,0:T(8,128)(2,1)S(1)}, u32[]{:S(2)}, u32[]{:S(2)}) collective-permute-start(bf16[48,3072]{1,0:T(8,128)(2,1)} %get-tuple-element.45), channel_id=1, source_target_pairs={{2,8},{3,9},{4,14},{5,15},{10,16},{11,17},{12,22},{13,23},{18,24},... | collective-permute-start | bytes 884744 | tf_op jit(solution)/shard_map/ppermute | solution.py:40
  175.4 30.6 %collective-permute-start.6 = (bf16[96,3072]{1,0:T(8,128)(2,1)S(1)}, bf16[96,3072]{1,0:T(8,128)(2,1)S(1)}, u32[]{:S(2)}, u32[]{:S(2)}) collective-permute-start(bf16[96,3072]{1,0:T(8,128)(2,1)S(1)} %get-tuple-element.27), channel_id=1, source_target_pairs={{0,8},{1,9},{2,10},{3,11},{4,12},{5,13},{6,14},{7,15},{8,16},{9,17... | collective-permute-start | bytes 1769480 | tf_op jit(solution)/shard_map/ppermute | solution.py:40
  177.8 26.9 %collective-permute-start.24 = (bf16[48,3072]{1,0:T(8,128)(2,1)}, bf16[48,3072]{1,0:T(8,128)(2,1)S(1)}, u32[]{:S(2)}, u32[]{:S(2)}) collective-permute-start(bf16[48,3072]{1,0:T(8,128)(2,1)} %get-tuple-element.49), channel_id=1, source_target_pairs={{2,8},{3,9},{4,14},{5,15},{10,16},{11,17},{12,22},{13,23},{18,24},... | collective-permute-start | bytes 884744 | tf_op jit(solution)/shard_map/ppermute | solution.py:40
  179.1 27.2 %collective-permute-start.28 = (bf16[48,3072]{1,0:T(8,128)(2,1)S(1)}, bf16[48,3072]{1,0:T(8,128)(2,1)S(1)}, u32[]{:S(2)}, u32[]{:S(2)}) collective-permute-start(bf16[48,3072]{1,0:T(8,128)(2,1)S(1)} %get-tuple-element.48), channel_id=1, source_target_pairs={{2,13},{3,12},{4,11},{5,10},{10,21},{11,20},{12,19},{13,18},{18,29... | collective-permute-start | bytes 884744 | tf_op jit(solution)/shard_map/ppermute | solution.py:40
  179.8 26.5 %collective-permute-start.26 = (bf16[48,3072]{1,0:T(8,128)(2,1)S(1)}, bf16[48,3072]{1,0:T(8,128)(2,1)S(1)}, u32[]{:S(2)}, u32[]{:S(2)}) collective-permute-start(bf16[48,3072]{1,0:T(8,128)(2,1)S(1)} %get-tuple-element.44), channel_id=1, source_target_pairs={{2,13},{3,12},{4,11},{5,10},{10,21},{11,20},{12,19},{13,18},{18,29... | collective-permute-start | bytes 884744 | tf_op jit(solution)/shard_map/ppermute | solution.py:40
  201.3 11.2 %collective-permute-start.27 = (bf16[48,3072]{1,0:T(8,128)(2,1)}, bf16[48,3072]{1,0:T(8,128)(2,1)S(1)}, u32[]{:S(2)}, u32[]{:S(2)}) collective-permute-start(bf16[48,3072]{1,0:T(8,128)(2,1)} %get-tuple-element.46), channel_id=1, source_target_pairs={{2,9},{3,8},{4,15},{5,14},{10,17},{11,16},{12,23},{13,22},{18,25},... | collective-permute-start | bytes 884744 | tf_op jit(solution)/shard_map/ppermute | solution.py:40
  204.7 14.1 %collective-permute-start.29 = (bf16[48,3072]{1,0:T(8,128)(2,1)}, bf16[48,3072]{1,0:T(8,128)(2,1)S(1)}, u32[]{:S(2)}, u32[]{:S(2)}) collective-permute-start(bf16[48,3072]{1,0:T(8,128)(2,1)} %get-tuple-element.50), channel_id=1, source_target_pairs={{2,9},{3,8},{4,15},{5,14},{10,17},{11,16},{12,23},{13,22},{18,25},... | collective-permute-start | bytes 884744 | tf_op jit(solution)/shard_map/ppermute | solution.py:40
  206.0 27.5 %collective-permute-start.25 = (bf16[96,3072]{1,0:T(8,128)(2,1)S(1)}, bf16[96,3072]{1,0:T(8,128)(2,1)S(1)}, u32[]{:S(2)}, u32[]{:S(2)}) collective-permute-start(bf16[96,3072]{1,0:T(8,128)(2,1)S(1)} %get-tuple-element.28), channel_id=1, source_target_pairs={{0,9},{1,8},{2,11},{3,10},{4,13},{5,12},{6,15},{7,14},{8,17},{9,16... | collective-permute-start | bytes 1769480 | tf_op jit(solution)/shard_map/ppermute | solution.py:40
where the time goes:
time: 236 us; the launch traced here: 235 us
  waiting for transfers between devices  149 us (63%)
  starting transfers between devices  35.6 us (15%)
  Pallas kernels  31.2 us (13%)
  local copies, waits for them, and re-layouts  12.8 us (5%)
  other arithmetic  5.71 us (2%)
    ppermute x16, waiting for transfers between devices, along_line(): return lax.ppermute(value, 'tensor', full)  97.3 us
    ppermute x10, waiting for transfers between devices, to_next_phase(): return lax.ppermute(value, ('segment', 'tensor'), full)  50.1 us
    pallas_call x3, Pallas kernels, ffn(): pl.pallas_call(functools.partial(ffn_kernel, layout), out_shape=[jax.Shap...  31.2 us
    ppermute x16, starting transfers between devices, along_line(): return lax.ppermute(value, 'tensor', full)  25.1 us
    ppermute x10, starting transfers between devices, to_next_phase(): return lax.ppermute(value, ('segment', 'tensor'), full)  9.41 us
    unnamed x36, local copies, waits for them, and re-layouts  5.74 us
  transfers between devices with their start and end apart: 30, of which 11 were waited for; matrix products, arithmetic and copies ran while one was open for 3% of the time, Pallas kernels for 13%

commit v1 on v0

--- a/solution.py
+++ b/solution.py
@@ -16,6 +16,7 @@
 MIDDLE = [(1, 2), (2, 1)]
 OUTWARD = [(1, 0), (2, 3)]
 INWARD = [(0, 1), (3, 2)]
+ENDS = [(0, 0), (3, 3)]
 STAY = [(0, 0), (1, 1), (2, 2), (3, 3)]
 
 
@@ -40,9 +41,9 @@
     return lax.ppermute(value, ("segment", "tensor"), full)
 
 
-def ffn_kernel(layout, *refs):
+def ffn_kernel(layout, out_rows, *refs):
     n_in = sum(choices for _, choices in layout)
-    n_out = len(layout)
+    n_out = len(out_rows)
     meta, slot_rows, slot_gates = refs[:3]
     x_refs = refs[3 : 3 + n_in]
     weights = refs[3 + n_in : 9 + n_in]
@@ -91,16 +92,12 @@
             def _(here=here, ref=first_ref):
                 x[here, :] = ref[...]
 
-        half_rows = rows // CORES
-        for half in range(CORES):
-            tokens = meta[1 + CORES * block + half] + lax.broadcasted_iota(
-                jnp.int32, (half_rows, slot_rows.shape[1]), 0
-            )
-            named = jnp.where(slot_rows[...] == tokens, slot_gates[...], 0.0)
-            column = jnp.sum(named, axis=1, keepdims=True)
-            gate[pl.ds(start + half * half_rows, half_rows), :] = jnp.broadcast_to(
-                column, (half_rows, gate.shape[1])
-            )
+        tokens = meta[1 + block] + lax.broadcasted_iota(
+            jnp.int32, (rows, slot_rows.shape[1]), 0
+        )
+        named = jnp.where(slot_rows[...] == tokens, slot_gates[...], 0.0)
+        column = jnp.sum(named, axis=1, keepdims=True)
+        gate[here, :] = jnp.broadcast_to(column, (rows, gate.shape[1]))
         start += rows
         at += choices
 
@@ -117,12 +114,12 @@
         y = jnp.dot(h[...], wd[column], preferred_element_type=F32)
         y = (y * gate[:, :1]).astype(BF16)
         start = 0
-        for (rows, _), out in zip(layout, outs):
+        for rows, out in zip(out_rows, outs):
             out[:, span] = y[start : start + rows, :]
             start += rows
 
 
-def ffn(meta, slot_rows, slot_gates, blocks, weights):
+def ffn(meta, slot_rows, slot_gates, blocks, weights, out_rows):
     layout = tuple((block[0].shape[0], len(block)) for block in blocks)
     features, hidden_units = weights[0].shape
     total = sum(rows for rows, _ in layout)
@@ -134,12 +131,12 @@
     vmem = pl.BlockSpec(memory_space=pltpu.VMEM)
     flat = [choice for block in blocks for choice in block]
     return pl.pallas_call(
-        functools.partial(ffn_kernel, layout),
-        out_shape=[jax.ShapeDtypeStruct((rows, features), BF16) for rows, _ in layout],
+        functools.partial(ffn_kernel, layout, out_rows),
+        out_shape=[jax.ShapeDtypeStruct((rows, features), BF16) for rows in out_rows],
         in_specs=[pl.BlockSpec(memory_space=pltpu.SMEM), vmem, vmem]
         + [vmem] * len(flat)
         + [any_space] * 6,
-        out_specs=[vmem] * len(layout),
+        out_specs=[vmem] * len(out_rows),
         scratch_shapes=[
             pltpu.VMEM((total, features), BF16),
             pltpu.VMEM((total, CORES * hidden_units), BF16),
@@ -153,9 +150,7 @@
         ],
         compiler_params=pltpu.CompilerParams(vmem_limit_bytes=44 * 1024 * 1024),
         cost_estimate=pl.CostEstimate(
-            flops=12 * total * features * hidden_units,
-            bytes_accessed=12 * features * hidden_units,
-            transcendentals=total * CORES * hidden_units,
+            flops=total * features, bytes_accessed=total * features, transcendentals=0
         ),
     )(meta, slot_rows, slot_gates, *flat, *weights)
 
@@ -164,13 +159,17 @@
     return sum(value.astype(F32) for value in values).astype(BF16)
 
 
-def staged(hidden, gate_weight, up_weight, down_weight, block_rows, slot_gate, chunks):
+def after(value, *events):
+    return lax.optimization_barrier((value, *events))[0]
+
+
+def staged(hidden, gate_weight, up_weight, down_weight, block_rows, slot_gate, parts):
     rows_here, features = hidden.shape[2], hidden.shape[3]
     slots = block_rows.shape[2] * block_rows.shape[3]
     index = lax.axis_index("tensor")
     core, chip = index % CORES, index // CORES
     right = chip >= CHIPS // 2
-    inner = jnp.logical_and(chip > 0, chip < CHIPS - 1)
+    inner = jnp.logical_and(chip > 0, chip < CHIPS - 1).astype(jnp.int32)
 
     mine = lax.dynamic_index_in_dim(hidden[0], core, 0, keepdims=False)
     theirs = lax.dynamic_index_in_dim(hidden[0], 1 - core, 0, keepdims=False)
@@ -183,84 +182,99 @@
     )
     weights = own_weights + [across_cores(weight) for weight in own_weights]
 
-    spans, start = [], 0
-    for size in chunks:
-        spans.append((start, size))
-        start += size
-
-    def token(mirrored_block, half, offset):
-        block = jnp.where(right, CHIPS - 1 - mirrored_block, mirrored_block)
-        owner = block * CORES + jnp.where(half == 0, core, 1 - core)
-        return owner * rows_here + offset
-
-    def meta_of(blocks, flag):
-        values = [flag.astype(jnp.int32)]
-        for mirrored_block, offset in blocks:
-            values += [token(mirrored_block, half, offset) for half in range(CORES)]
+    chunks = []
+    for half, sizes in enumerate(parts):
+        start = 0
+        for size in sizes:
+            chunks.append((half, start, size))
+            start += size
+    pieces = [
+        (mine if half == 0 else other)[start : start + size] for half, start, size in chunks
+    ]
+    last = len(chunks)
+    at_inner = inner == 1
+
+    def meta_of(runs):
+        values = [inner]
+        for mirrored_block, chunk in runs:
+            half, start, _ = chunks[chunk]
+            block = jnp.where(right, CHIPS - 1 - mirrored_block, mirrored_block)
+            owner = block * CORES + (core if half == 0 else 1 - core)
+            values.append(owner * rows_here + start)
         return jnp.stack(values).astype(jnp.int32)
 
-    own_block = inner.astype(jnp.int32)
-    near_block = 1 - own_block
-
-    own = jnp.concatenate([mine, other], axis=0)
-    pieces = [
-        jnp.concatenate([mine[o : o + n], other[o : o + n]], axis=0) for o, n in spans
+    def expert(runs, inputs, out_rows):
+        return ffn(meta_of(runs), slot_rows, slot_gates, inputs, weights, out_rows)
+
+    near, second_in, third_in, second_out, third_out = ([None] * last for _ in range(5))
+    for k in range(last):
+        near[k] = along_line(pieces[k], NEAR)
+    second_in[0] = along_line(after(pieces[0], other), MIDDLE)
+    third_in[0] = along_line(after(near[0], second_in[0]), MIDDLE)
+    second_out[0] = along_line(after(second_in[0], near[0]), NEAR)
+
+    ready = [third_in[0]] + near[1:]
+    near_in = [after(pieces[0], second_out[0], *ready)] + pieces[1:]
+    out = expert(
+        [(inner, k) for k in range(last)] + [(1 - inner, k) for k in range(last)],
+        [(piece,) for piece in near_in] + [(value,) for value in near],
+        [chunk[2] for chunk in chunks] * 2,
+    )
+    own_part, near_part = out[:last], out[last:]
+    third_out[0] = along_line(after(third_in[0], *near), NEAR)
+    for k in range(1, last):
+        if k > 1:
+            ready = [third_in[k - 1]]
+        second_in[k] = along_line(after(pieces[k], *ready), MIDDLE)
+        third_in[k] = along_line(after(near[k], *ready), MIDDLE)
+        second_out[k] = along_line(after(second_in[k], own_part[0]), OUTWARD)
+        third_out[k] = along_line(after(third_in[k], own_part[0]), OUTWARD)
+
+    base = [
+        to_next_phase(
+            jnp.concatenate(
+                [add(pieces[k], own_part[k]) for k in range(last) if chunks[k][0] == half]
+            ),
+            STAY,
+            half,
+        )
+        for half in range(CORES)
     ]
 
-    near = along_line(own, NEAR)
-    second_at_inner = [along_line(piece, MIDDLE) for piece in pieces]
-    second_at_outer = [along_line(piece, OUTWARD) for piece in second_at_inner]
-    near_pieces = [
-        jnp.concatenate(
-            [near[o : o + n], near[rows_here + o : rows_here + o + n]], axis=0
+    handed = [[], []]
+    over = to_pair = None
+    for k, (half, start, size) in enumerate(chunks):
+        events = [own_part[0]]
+        if k + 1 < last:
+            events += [second_in[k + 1], third_in[k + 1]]
+        inputs = [
+            (after(second_out[k], *events), second_in[k]),
+            (third_out[k], third_in[k]),
+        ]
+        if k + 1 < last:
+            part = expert([(2, k), (3, k)], inputs, [2 * size])[0]
+            total = add(part, along_line(part, INWARD))
+            sum2, sum3 = total[:size], total[size:]
+        else:
+            part2, part3 = expert([(2, k), (3, k)], inputs, [size, size])
+            sum3 = add(part3, along_line(part3, INWARD))
+            if k > 0:
+                part2, sum3 = after(part2, over), after(sum3, for_pair)
+            sum2 = add(part2, along_line(part2, INWARD))
+        sum2 = jnp.where(at_inner, sum2, 0)
+        over = along_line(sum3, MIDDLE)
+        for_pair = add(near_part[k], jnp.where(at_inner, over, 0))
+        if k > 0:
+            for_pair = after(for_pair, to_pair)
+        to_pair = to_next_phase(for_pair, NEAR, half)
+        handed[half].append(
+            add(
+                base[half][start : start + size],
+                to_next_phase(sum2, MIDDLE + ENDS, half),
+                to_pair,
+            )
         )
-        for o, n in spans
-    ]
-    third_at_inner = [along_line(piece, MIDDLE) for piece in near_pieces]
-    third_at_outer = [along_line(piece, OUTWARD) for piece in third_at_inner]
-
-    own_part, near_part = ffn(
-        meta_of([(own_block, 0), (near_block, 0)], jnp.int32(0)),
-        slot_rows,
-        slot_gates,
-        [(own,), (near,)],
-        weights,
-    )
-    from_end = along_line(near_part, INWARD)
-
-    base = add(own, own_part, from_end)
-    base_same = to_next_phase(base[:rows_here], STAY, 0)
-    base_cross = to_next_phase(base[rows_here:], STAY, 1)
-
-    same, cross = [], []
-    for (o, n), a2, b2, a3, b3 in zip(
-        spans, second_at_outer, second_at_inner, third_at_outer, third_at_inner
-    ):
-        part2, part3 = ffn(
-            meta_of([(2, o), (3, o)], inner),
-            slot_rows,
-            slot_gates,
-            [(a2, b2), (a3, b3)],
-            weights,
-        )
-        sum3 = add(part3, along_line(part3, INWARD))
-        sum2 = add(part2, along_line(part2, INWARD))
-        over = along_line(sum3, MIDDLE)
-        for_end = add(
-            jnp.concatenate(
-                [near_part[o : o + n], near_part[rows_here + o : rows_here + o + n]], axis=0
-            ),
-            over,
-        )
-        got_same = [base_same[o : o + n]]
-        got_cross = [base_cross[o : o + n]]
-        for value, pairs in ((sum2, MIDDLE), (for_end, OUTWARD)):
-            got_same.append(to_next_phase(value[:n], pairs, 0))
-            got_cross.append(to_next_phase(value[n:], pairs, 1))
-        same.append(add(*got_same))
-        cross.append(add(*got_cross))
-    same = jnp.concatenate(same, axis=0)
-    cross = jnp.concatenate(cross, axis=0)
+    same, cross = (jnp.concatenate(half, axis=0) for half in handed)
     low = core == 0
     return jnp.stack([jnp.where(low, same, cross), jnp.where(low, cross, same)])[None]
 
@@ -298,11 +312,7 @@
         or rows_here % 32 != 0
     ):
         return whole_gather(*args)
-    return staged(*args, chunks=CHUNKS(rows_here))
-
-
-def CHUNKS(rows):
-    return [rows // 2, rows // 2]
+    return staged(*args, parts=[[rows_here], [rows_here]])
 
 
 def solution(mesh):

time: 236 us -> 191 us (0.81)
  waiting for transfers between devices: 149 us -> 93.4 us
  starting transfers between devices: 35.6 us -> 50.6 us
  local copies, waits for them, and re-layouts: 12.8 us -> 6.73 us
    ppermute x16 -> x15, waiting for transfers between devices: 97.3 us -> 65.5 us  [along_line(): return lax.ppermute(value, 'tensor', full)]
    ppermute x10 -> x6, waiting for transfers between devices: 50.1 us -> 26.2 us  [to_next_phase(): return lax.ppermute(value, ('segment', 'tensor'), full)]
    ppermute x16 -> x15, starting transfers between devices: 25.1 us -> 34.9 us  [along_line(): return lax.ppermute(value, 'tensor', full)]
    ppermute x10 -> x6, starting transfers between devices: 9.41 us -> 14.3 us  [to_next_phase(): return lax.ppermute(value, ('segment', 'tensor'), full)]
    slice x9 -> x0, local copies, waits for them, and re-layouts: 4.59 us -> none  [the longest x4 3.22 us: staged(): got_same.append(to_next_phase(value[:n], pairs, 0))]
    concatenate x7 -> x0, other arithmetic: 2.8 us -> none  [the longest x1 1.36 us: staged(): own = jnp.concatenate([mine, other], axis=0)]
    unnamed x36 -> x16, local copies, waits for them, and re-layouts: 5.74 us -> 4.61 us
  transfers between devices with their start and end apart: 30 -> 25, of which waited for: 11 -> 11; matrix products, arithmetic and copies ran while one was open for 3% -> 3% of each run, Pallas kernels for 13% -> 16%
where the time goes in v1:
time: 191 us; the launch traced here: 190 us
  waiting for transfers between devices  93.4 us (49%)
  starting transfers between devices  50.6 us (26%)
  Pallas kernels  31.2 us (16%)
  other arithmetic  7.48 us (4%)
  local copies, waits for them, and re-layouts  6.73 us (4%)
    ppermute x15, waiting for transfers between devices, along_line(): return lax.ppermute(value, 'tensor', full)  65.5 us
    ppermute x15, starting transfers between devices, along_line(): return lax.ppermute(value, 'tensor', full)  34.9 us
    pallas_call x3, Pallas kernels, ffn(): pl.pallas_call(functools.partial(ffn_kernel, layout, out_rows), out_shape...  31.2 us
    ppermute x6, waiting for transfers between devices, to_next_phase(): return lax.ppermute(value, ('segment', 'tensor'), full)  26.2 us
    ppermute x6, starting transfers between devices, to_next_phase(): return lax.ppermute(value, ('segment', 'tensor'), full)  14.3 us
    unnamed x16, local copies, waits for them, and re-layouts  4.61 us
  transfers between devices with their start and end apart: 25, of which 11 were waited for; matrix products, arithmetic and copies ran while one was open for 3% of the time, Pallas kernels for 16%

profile of v1, /device:TPU:0, one launch (start us, length us, event | category | flops | bytes accessed | tf_op | source)
XLA Modules:
  0.0 189.6 jit_solution(334306648585385731)
XLA Ops:
  0.0 1.3 dynamic-slice_bitcast_fusion
  1.3 0.5 collective-permute-start
  1.9 1.6 collective-permute-done.refs_4_
  3.5 0.4 collective-permute-start.6
  3.9 0.1 collective-permute-start.7
  4.0 0.4 collective-permute-start.8
  4.4 2.7 %collective-permute-start.2 = (bf16[96,3072]{1,0:T(8,128)(2,1)S(1)}, bf16[96,3072]{1,0:T(8,128)(2,1)S(1)}, u32[]{:S(2)}, u32[]{:S(2)}) collective-permute-start(bf16[96,3072]{1,0:T(8,128)(2,1)S(1)} %get-tuple-element.33.refs_3_), channel_id=1, source_target_pairs={{0,2},{1,3},{2,0},{3,1},{4,6},{5,7},{6,4},{7,5},{8,10},{9,11},{10,... | collective-permute-start | bytes 1769480 | tf_op jit(solution)/shard_map/ppermute | solution.py:25
  7.1 0.7 collective-permute-start.1
  7.8 13.2 %collective-permute-done.2.refs_5_ = bf16[96,3072]{1,0:T(8,128)(2,1)S(1)} collective-permute-done((bf16[96,3072]{1,0:T(8,128)(2,1)S(1)}, bf16[96,3072]{1,0:T(8,128)(2,1)S(1)}, u32[]{:S(2)}, u32[]{:S(2)}) %collective-permute-start.2) | collective-permute-done | bytes 589856 | tf_op jit(solution)/shard_map/ppermute | solution.py:25
  20.9 1.7 collective-permute-start.5
  22.7 0.0 collective-permute-done.1.refs_4_
  22.7 0.7 collective-permute-start.4
  23.4 0.0 copy-start.4
  23.4 0.8 copy-done.4
  24.2 11.9 %collective-permute-done.5.refs_6_ = bf16[96,3072]{1,0:T(8,128)(2,1)} collective-permute-done((bf16[96,3072]{1,0:T(8,128)(2,1)S(1)}, bf16[96,3072]{1,0:T(8,128)(2,1)}, u32[]{:S(2)}, u32[]{:S(2)}) %collective-permute-start.5) | collective-permute-done | bytes 589856 | tf_op jit(solution)/shard_map/ppermute | solution.py:25
  36.1 1.5 collective-permute-start.3
  37.6 0.0 collective-permute-done.4.refs_6_
  37.6 0.7 collective-permute-start.11
  38.3 12.0 %collective-permute-done.3.refs_3_ = bf16[96,3072]{1,0:T(8,128)(2,1)S(1)} collective-permute-done((bf16[96,3072]{1,0:T(8,128)(2,1)S(1)}, bf16[96,3072]{1,0:T(8,128)(2,1)S(1)}, u32[]{:S(2)}, u32[]{:S(2)}) %collective-permute-start.3) | collective-permute-done | bytes 589856 | tf_op jit(solution)/shard_map/ppermute | solution.py:25
  50.2 0.8 copy-done.6
  51.1 0.7 collective-permute-start.10
  51.8 4.1 %collective-permute-start.12 = (bf16[96,3072]{1,0:T(8,128)(2,1)S(1)}, bf16[96,3072]{1,0:T(8,128)(2,1)}, u32[]{:S(2)}, u32[]{:S(2)}) collective-permute-start(bf16[96,3072]{1,0:T(8,128)(2,1)S(1)} %collective-permute-done.4.refs_6_), channel_id=1, source_target_pairs={{0,2},{1,3},{2,0},{3,1},{4,6},{5,7},{6,4},{7,5},{8,10},{9,11},{10,... | collective-permute-start | bytes 1769480 | tf_op jit(solution)/shard_map/ppermute | solution.py:25
  55.9 0.1 stack.52.refs_0_
  55.9 0.1 pad_add_fusion.1.refs_0_
  56.0 0.1 pad_add_fusion.refs_0_
  56.1 0.7 dynamic-slice_bitcast_fusion.2.refs_2_
  56.8 0.0 collective-permute-done.7.refs_11_
  56.8 0.0 copy-start.1
  56.8 1.9 copy-done.1
  58.7 1.1 copy-done.5
  59.8 13.3 %shard_map.64 = (bf16[96,3072]{1,0:T(8,128)(2,1)S(1)}, bf16[96,3072]{1,0:T(8,128)(2,1)S(1)}, bf16[96,3072]{1,0:T(8,128)(2,1)S(1)}, bf16[96,3072]{1,0:T(8,128)(2,1)S(1)}) custom-call(s32[5]{0:T(128)S(1)} %stack.52.refs_0_, s32[1,768]{1,0:T(1,128)S(1)} %dynamic-slice_bitcast_fusion.3.refs_1_, f32[1,768]{1,0:T(1,128)S(1)} %dynamic-slice_bitcast_fusion.2.refs_2_, ...), custom_call_target="tpu_custom_call" | custom-call | flops 1179648 | bytes 1179648 | tf_op jit(solution)/shard_map/pallas_call | solution.py:133
  73.1 1.3 collective-permute-start.18
  74.4 1.3 collective-permute-start.19
  75.7 0.0 collective-permute-done.12.refs_5_
  75.7 9.2 %shard_map.65 = bf16[192,3072]{1,0:T(8,128)(2,1)S(1)} custom-call(s32[3]{0:T(128)S(1)} %pad_add_fusion.refs_0_, s32[1,768]{1,0:T(1,128)S(1)} %dynamic-slice_bitcast_fusion.3.refs_1_, f32[1,768]{1,0:T(1,128)S(1)} %dynamic-slice_bitcast_fusion.2.refs_2_, bf16[96,3072]{1,0:T(8,128)(2,1)S(1)} %copy-done.7, bf16[96,3072]{1,0:T(8,128)(2,1)S(1)} %collective-permute-done.1.refs_4_, ...), custom_call_target="tpu_custom_call" | custom-call | flops 589824 | bytes 589824 | tf_op jit(solution)/shard_map/pallas_call | solution.py:133
  84.9 4.7 %collective-permute-start.13 = (bf16[192,3072]{1,0:T(8,128)(2,1)S(1)}, bf16[192,3072]{1,0:T(8,128)(2,1)S(1)}, u32[]{:S(2)}, u32[]{:S(2)}) collective-permute-start(bf16[192,3072]{1,0:T(8,128)(2,1)S(1)} %shard_map.65), channel_id=1, source_target_pairs={{0,2},{1,3},{6,4},{7,5},{8,10},{9,11},{14,12},{15,13},{16,18},{17,... | collective-permute-start | bytes 3538952 | tf_op jit(solution)/shard_map/ppermute | solution.py:25
  89.7 1.0 add_convert_fusion.5
  90.6 0.0 collective-permute-start.17
  90.6 1.0 add_convert_fusion.8
  91.6 1.5 collective-permute-start.9
  93.1 0.0 collective-permute-done.18.refs_3_
  93.1 6.9 %collective-permute-done.19.refs_5_ = bf16[96,3072]{1,0:T(8,128)(2,1)S(1)} collective-permute-done((bf16[96,3072]{1,0:T(8,128)(2,1)S(1)}, bf16[96,3072]{1,0:T(8,128)(2,1)S(1)}, u32[]{:S(2)}, u32[]{:S(2)}) %collective-permute-start.19) | collective-permute-done | bytes 589856 | tf_op jit(solution)/shard_map/ppermute | solution.py:25
  100.0 8.7 %shard_map.66 = (bf16[96,3072]{1,0:T(8,128)(2,1)S(1)}, bf16[96,3072]{1,0:T(8,128)(2,1)S(1)}) custom-call(s32[3]{0:T(128)S(1)} %pad_add_fusion.1.refs_0_, s32[1,768]{1,0:T(1,128)S(1)} %dynamic-slice_bitcast_fusion.3.refs_1_, f32[1,768]{1,0:T(1,128)S(1)} %dynamic-slice_bitcast_fusion.2.refs_2_, bf16[96,3072]{1,0:T(8,128)(2,1)S(1)} %collective-permute-done.18.refs_3_, ...), custom_call_target="tpu_custom_call" | custom-call | flops 589824 | bytes 589824 | tf_op jit(solution)/shard_map/pallas_call | solution.py:133
  108.7 1.5 collective-permute-start.22
  110.2 5.8 %collective-permute-done.13 = bf16[192,3072]{1,0:T(8,128)(2,1)S(1)} collective-permute-done((bf16[192,3072]{1,0:T(8,128)(2,1)S(1)}, bf16[192,3072]{1,0:T(8,128)(2,1)S(1)}, u32[]{:S(2)}, u32[]{:S(2)}) %collective-permute-start.13) | collective-permute-done | bytes 1179680 | tf_op jit(solution)/shard_map/ppermute | solution.py:25
  116.0 0.4 add_convert_fusion
  116.4 0.9 slice_select_fusion
  117.3 0.7 collective-permute-start.15
  118.0 6.5 %collective-permute-done.22 = bf16[96,3072]{1,0:T(8,128)(2,1)S(1)} collective-permute-done((bf16[96,3072]{1,0:T(8,128)(2,1)S(1)}, bf16[96,3072]{1,0:T(8,128)(2,1)S(1)}, u32[]{:S(2)}, u32[]{:S(2)}) %collective-permute-start.22) | collective-permute-done | bytes 589856 | tf_op jit(solution)/shard_map/ppermute | solution.py:25
  124.5 0.1 add_convert_fusion.3
  124.6 1.6 collective-permute-start.14
  126.2 11.9 %collective-permute-start.20 = (bf16[96,3072]{1,0:T(8,128)(2,1)S(1)}, bf16[96,3072]{1,0:T(8,128)(2,1)S(1)}, u32[]{:S(2)}, u32[]{:S(2)}) collective-permute-start(bf16[96,3072]{1,0:T(8,128)(2,1)S(1)} %get-tuple-element.48), channel_id=1, source_target_pairs={{0,2},{1,3},{6,4},{7,5},{8,10},{9,11},{14,12},{15,13},{16,18},{17,... | collective-permute-start | bytes 1769480 | tf_op jit(solution)/shard_map/ppermute | solution.py:25
  138.1 0.2 add_convert_fusion.7
  138.3 0.3 collective-permute-start.16
  138.6 9.4 %collective-permute-done.20 = bf16[96,3072]{1,0:T(8,128)(2,1)S(1)} collective-permute-done((bf16[96,3072]{1,0:T(8,128)(2,1)S(1)}, bf16[96,3072]{1,0:T(8,128)(2,1)S(1)}, u32[]{:S(2)}, u32[]{:S(2)}) %collective-permute-start.20) | collective-permute-done | bytes 589856 | tf_op jit(solution)/shard_map/ppermute | solution.py:25
  148.0 0.7 collective-permute-start.23
  148.7 1.0 fusion
  149.7 1.0 add_convert_fusion.2
  150.7 4.2 %collective-permute-done.16 = bf16[96,3072]{1,0:T(8,128)(2,1)S(1)} collective-permute-done((bf16[96,3072]{1,0:T(8,128)(2,1)S(1)}, bf16[96,3072]{1,0:T(8,128)(2,1)S(1)}, u32[]{:S(2)}, u32[]{:S(2)}) %collective-permute-start.16) | collective-permute-done | bytes 589856 | tf_op jit(solution)/shard_map/ppermute | solution.py:41
  154.9 10.9 %collective-permute-start.24 = (bf16[96,3072]{1,0:T(8,128)(2,1)}, bf16[96,3072]{1,0:T(8,128)(2,1)S(1)}, u32[]{:S(2)}, u32[]{:S(2)}) collective-permute-start(bf16[96,3072]{1,0:T(8,128)(2,1)} %add_convert_fusion.2), channel_id=1, source_target_pairs={{0,11},{1,10},{2,9},{3,8},{4,15},{5,14},{6,13},{7,12},{8,19},{9,18... | collective-permute-start | bytes 1769480 | tf_op jit(solution)/shard_map/ppermute | solution.py:41
  165.8 0.5 collective-permute-done.21
  166.3 21.6 %collective-permute-done.24 = bf16[96,3072]{1,0:T(8,128)(2,1)S(1)} collective-permute-done((bf16[96,3072]{1,0:T(8,128)(2,1)}, bf16[96,3072]{1,0:T(8,128)(2,1)S(1)}, u32[]{:S(2)}, u32[]{:S(2)}) %collective-permute-start.24) | collective-permute-done | bytes 589856 | tf_op jit(solution)/shard_map/ppermute | solution.py:41
  187.9 0.6 select_bitcast_fusion.1
  188.5 1.1 maximum_bitcast_fusion
  (21 shorter events, 0.1 us)
Async XLA Ops:
  0.0 56.1 %copy-start = (s32[1,2,6,128]{3,1,2,0:T(2,128)S(1)}, s32[1,2,6,128]{3,1,2,0:T(2,128)}, u32[]{:S(2)}) copy-start(s32[1,2,6,128]{3,1,2,0:T(2,128)} %param.10) | copy-start | bytes 18436
  1.3 2.1 %collective-permute-start = (bf16[96,3072]{1,0:T(8,128)(2,1)S(1)}, bf16[96,3072]{1,0:T(8,128)(2,1)S(1)}, u32[]{:S(2)}, u32[]{:S(2)}) collective-permute-start(bf16[96,3072]{1,0:T(8,128)(2,1)S(1)} %get-tuple-element.57), channel_id=1, source_target_pairs={{0,1},{1,0},{2,3},{3,2},{4,5},{5,4},{6,7},{7,6},{8,9},{9,8},{10,11... | collective-permute-start | bytes 1769480 | tf_op jit(solution)/shard_map/ppermute | solution.py:30
  3.5 48.3 %collective-permute-start.6 = (bf16[3072,512]{1,0:T(8,128)(2,1)}, bf16[3072,512]{1,0:T(8,128)(2,1)}, u32[]{:S(2)}, u32[]{:S(2)}) collective-permute-start(bf16[3072,512]{1,0:T(8,128)(2,1)} %bitcast.26), channel_id=1, source_target_pairs={{0,1},{1,0},{2,3},{3,2},{4,5},{5,4},{6,7},{7,6},{8,9},{9,8},{10,11... | collective-permute-start | bytes 9437192 | tf_op jit(solution)/shard_map/ppermute | solution.py:30
  3.9 53.0 %collective-permute-start.7 = (bf16[3072,512]{1,0:T(8,128)(2,1)}, bf16[3072,512]{1,0:T(8,128)(2,1)}, u32[]{:S(2)}, u32[]{:S(2)}) collective-permute-start(bf16[3072,512]{1,0:T(8,128)(2,1)} %bitcast.30), channel_id=1, source_target_pairs={{0,1},{1,0},{2,3},{3,2},{4,5},{5,4},{6,7},{7,6},{8,9},{9,8},{10,11... | collective-permute-start | bytes 9437192 | tf_op jit(solution)/shard_map/ppermute | solution.py:30
  4.0 52.8 %collective-permute-start.8 = (bf16[512,3072]{1,0:T(8,128)(2,1)}, bf16[512,3072]{1,0:T(8,128)(2,1)}, u32[]{:S(2)}, u32[]{:S(2)}) collective-permute-start(bf16[512,3072]{1,0:T(8,128)(2,1)} %bitcast.34), channel_id=1, source_target_pairs={{0,1},{1,0},{2,3},{3,2},{4,5},{5,4},{6,7},{7,6},{8,9},{9,8},{10,11... | collective-permute-start | bytes 9437192 | tf_op jit(solution)/shard_map/ppermute | solution.py:30
  4.4 16.6 %collective-permute-start.2 = (bf16[96,3072]{1,0:T(8,128)(2,1)S(1)}, bf16[96,3072]{1,0:T(8,128)(2,1)S(1)}, u32[]{:S(2)}, u32[]{:S(2)}) collective-permute-start(bf16[96,3072]{1,0:T(8,128)(2,1)S(1)} %get-tuple-element.33.refs_3_), channel_id=1, source_target_pairs={{0,2},{1,3},{2,0},{3,1},{4,6},{5,7},{6,4},{7,5},{8,10},{9,11},{10,... | collective-permute-start | bytes 1769480 | tf_op jit(solution)/shard_map/ppermute | solution.py:25
  7.1 15.6 %collective-permute-start.1 = (bf16[96,3072]{1,0:T(8,128)(2,1)S(1)}, bf16[96,3072]{1,0:T(8,128)(2,1)S(1)}, u32[]{:S(2)}, u32[]{:S(2)}) collective-permute-start(bf16[96,3072]{1,0:T(8,128)(2,1)S(1)} %get-tuple-element.33.refs_3_), channel_id=1, source_target_pairs={{2,4},{3,5},{4,2},{5,3},{10,12},{11,13},{12,10},{13,11},{18,20},{1... | collective-permute-start | bytes 1769480 | tf_op jit(solution)/shard_map/ppermute | solution.py:25
  20.9 15.1 %collective-permute-start.5 = (bf16[96,3072]{1,0:T(8,128)(2,1)S(1)}, bf16[96,3072]{1,0:T(8,128)(2,1)}, u32[]{:S(2)}, u32[]{:S(2)}) collective-permute-start(bf16[96,3072]{1,0:T(8,128)(2,1)S(1)} %collective-permute-done.refs_4_), channel_id=1, source_target_pairs={{0,2},{1,3},{2,0},{3,1},{4,6},{5,7},{6,4},{7,5},{8,10},{9,11},{10,... | collective-permute-start | bytes 1769480 | tf_op jit(solution)/shard_map/ppermute | solution.py:25
  22.7 14.9 %collective-permute-start.4 = (bf16[96,3072]{1,0:T(8,128)(2,1)S(1)}, bf16[96,3072]{1,0:T(8,128)(2,1)S(1)}, u32[]{:S(2)}, u32[]{:S(2)}) collective-permute-start(bf16[96,3072]{1,0:T(8,128)(2,1)S(1)} %collective-permute-done.2.refs_5_), channel_id=1, source_target_pairs={{2,4},{3,5},{4,2},{5,3},{10,12},{11,13},{12,10},{13,11},{18,20},{1... | collective-permute-start | bytes 1769480 | tf_op jit(solution)/shard_map/ppermute | solution.py:25
  23.4 0.8 copy-start.4
  36.1 14.2 %collective-permute-start.3 = (bf16[96,3072]{1,0:T(8,128)(2,1)S(1)}, bf16[96,3072]{1,0:T(8,128)(2,1)S(1)}, u32[]{:S(2)}, u32[]{:S(2)}) collective-permute-start(bf16[96,3072]{1,0:T(8,128)(2,1)S(1)} %collective-permute-done.1.refs_4_), channel_id=1, source_target_pairs={{0,2},{1,3},{2,0},{3,1},{4,6},{5,7},{6,4},{7,5},{8,10},{9,11},{10,... | collective-permute-start | bytes 1769480 | tf_op jit(solution)/shard_map/ppermute | solution.py:25
  37.6 35.5 %collective-permute-start.11 = (bf16[96,3072]{1,0:T(8,128)(2,1)}, bf16[96,3072]{1,0:T(8,128)(2,1)S(1)}, u32[]{:S(2)}, u32[]{:S(2)}) collective-permute-start(bf16[96,3072]{1,0:T(8,128)(2,1)} %collective-permute-done.5.refs_6_), channel_id=1, source_target_pairs={{2,4},{3,5},{4,2},{5,3},{10,12},{11,13},{12,10},{13,11},{18,20},{1... | collective-permute-start | bytes 1769480 | tf_op jit(solution)/shard_map/ppermute | solution.py:25
  50.2 0.8 copy-start.6
  51.1 22.0 %collective-permute-start.10 = (bf16[96,3072]{1,0:T(8,128)(2,1)S(1)}, bf16[96,3072]{1,0:T(8,128)(2,1)S(1)}, u32[]{:S(2)}, u32[]{:S(2)}) collective-permute-start(bf16[96,3072]{1,0:T(8,128)(2,1)S(1)} %collective-permute-done.refs_4_), channel_id=1, source_target_pairs={{2,4},{3,5},{4,2},{5,3},{10,12},{11,13},{12,10},{13,11},{18,20},{1... | collective-permute-start | bytes 1769480 | tf_op jit(solution)/shard_map/ppermute | solution.py:25
  51.8 23.9 %collective-permute-start.12 = (bf16[96,3072]{1,0:T(8,128)(2,1)S(1)}, bf16[96,3072]{1,0:T(8,128)(2,1)}, u32[]{:S(2)}, u32[]{:S(2)}) collective-permute-start(bf16[96,3072]{1,0:T(8,128)(2,1)S(1)} %collective-permute-done.4.refs_6_), channel_id=1, source_target_pairs={{0,2},{1,3},{2,0},{3,1},{4,6},{5,7},{6,4},{7,5},{8,10},{9,11},{10,... | collective-permute-start | bytes 1769480 | tf_op jit(solution)/shard_map/ppermute | solution.py:25
  56.8 1.9 copy-start.1
  58.7 1.1 copy-start.5
  59.8 15.9 %copy-start.2 = (bf16[1,3072,512]{2,1,0:T(8,128)(2,1)S(1)}, bf16[1,3072,512]{2,1,0:T(8,128)(2,1)}, u32[]{:S(2)}) copy-start(bf16[1,3072,512]{2,1,0:T(8,128)(2,1)} %param.7) | copy-start | bytes 9437188
  59.8 15.9 %copy-start.3 = (bf16[1,3072,512]{2,1,0:T(8,128)(2,1)S(1)}, bf16[1,3072,512]{2,1,0:T(8,128)(2,1)}, u32[]{:S(2)}) copy-start(bf16[1,3072,512]{2,1,0:T(8,128)(2,1)} %param.8) | copy-start | bytes 9437188
  59.8 15.9 %copy-start.7 = (bf16[96,3072]{1,0:T(8,128)(2,1)S(1)}, bf16[96,3072]{1,0:T(8,128)(2,1)}, u32[]{:S(2)}) copy-start(bf16[96,3072]{1,0:T(8,128)(2,1)} %copy-done.6) | copy-start | bytes 1769476
  73.1 20.0 %collective-permute-start.18 = (bf16[96,3072]{1,0:T(8,128)(2,1)S(1)}, bf16[96,3072]{1,0:T(8,128)(2,1)S(1)}, u32[]{:S(2)}, u32[]{:S(2)}) collective-permute-start(bf16[96,3072]{1,0:T(8,128)(2,1)S(1)} %collective-permute-done.10.refs_4_), channel_id=1, source_target_pairs={{2,0},{3,1},{4,6},{5,7},{10,8},{11,9},{12,14},{13,15},{18,16},{19,... | collective-permute-start | bytes 1769480 | tf_op jit(solution)/shard_map/ppermute | solution.py:25
  74.4 25.6 %collective-permute-start.19 = (bf16[96,3072]{1,0:T(8,128)(2,1)S(1)}, bf16[96,3072]{1,0:T(8,128)(2,1)S(1)}, u32[]{:S(2)}, u32[]{:S(2)}) collective-permute-start(bf16[96,3072]{1,0:T(8,128)(2,1)S(1)} %collective-permute-done.11.refs_6_), channel_id=1, source_target_pairs={{2,0},{3,1},{4,6},{5,7},{10,8},{11,9},{12,14},{13,15},{18,16},{19,... | collective-permute-start | bytes 1769480 | tf_op jit(solution)/shard_map/ppermute | solution.py:25
  84.9 31.0 %collective-permute-start.13 = (bf16[192,3072]{1,0:T(8,128)(2,1)S(1)}, bf16[192,3072]{1,0:T(8,128)(2,1)S(1)}, u32[]{:S(2)}, u32[]{:S(2)}) collective-permute-start(bf16[192,3072]{1,0:T(8,128)(2,1)S(1)} %shard_map.65), channel_id=1, source_target_pairs={{0,2},{1,3},{6,4},{7,5},{8,10},{9,11},{14,12},{15,13},{16,18},{17,... | collective-permute-start | bytes 3538952 | tf_op jit(solution)/shard_map/ppermute | solution.py:25
  90.6 75.2 %collective-permute-start.17 = (bf16[96,3072]{1,0:T(8,128)(2,1)}, bf16[96,3072]{1,0:T(8,128)(2,1)S(1)}, u32[]{:S(2)}, u32[]{:S(2)}) collective-permute-start(bf16[96,3072]{1,0:T(8,128)(2,1)} %add_convert_fusion.5), channel_id=1, source_target_pairs={{0,9},{1,8},{2,11},{3,10},{4,13},{5,12},{6,15},{7,14},{8,17},{9,16... | collective-permute-start | bytes 1769480 | tf_op jit(solution)/shard_map/ppermute | solution.py:41
  91.6 74.2 %collective-permute-start.9 = (bf16[96,3072]{1,0:T(8,128)(2,1)}, bf16[96,3072]{1,0:T(8,128)(2,1)S(1)}, u32[]{:S(2)}, u32[]{:S(2)}) collective-permute-start(bf16[96,3072]{1,0:T(8,128)(2,1)} %add_convert_fusion.8), channel_id=1, source_target_pairs={{0,8},{1,9},{2,10},{3,11},{4,12},{5,13},{6,14},{7,15},{8,16},{9,17... | collective-permute-start | bytes 1769480 | tf_op jit(solution)/shard_map/ppermute | solution.py:41
  108.7 15.8 %collective-permute-start.22 = (bf16[96,3072]{1,0:T(8,128)(2,1)S(1)}, bf16[96,3072]{1,0:T(8,128)(2,1)S(1)}, u32[]{:S(2)}, u32[]{:S(2)}) collective-permute-start(bf16[96,3072]{1,0:T(8,128)(2,1)S(1)} %get-tuple-element.50), channel_id=1, source_target_pairs={{0,2},{1,3},{6,4},{7,5},{8,10},{9,11},{14,12},{15,13},{16,18},{17,... | collective-permute-start | bytes 1769480 | tf_op jit(solution)/shard_map/ppermute | solution.py:25
  117.3 8.9 %collective-permute-start.15 = (bf16[96,3072]{1,0:T(8,128)(2,1)S(1)}, bf16[96,3072]{1,0:T(8,128)(2,1)S(1)}, u32[]{:S(2)}, u32[]{:S(2)}) collective-permute-start(bf16[96,3072]{1,0:T(8,128)(2,1)S(1)} %get-tuple-element.56), channel_id=1, source_target_pairs={{2,4},{3,5},{4,2},{5,3},{10,12},{11,13},{12,10},{13,11},{18,20},{1... | collective-permute-start | bytes 1769480 | tf_op jit(solution)/shard_map/ppermute | solution.py:25
  124.6 41.2 %collective-permute-start.14 = (bf16[96,3072]{1,0:T(8,128)(2,1)}, bf16[96,3072]{1,0:T(8,128)(2,1)S(1)}, u32[]{:S(2)}, u32[]{:S(2)}) collective-permute-start(bf16[96,3072]{1,0:T(8,128)(2,1)} %get-tuple-element.55), channel_id=1, source_target_pairs={{2,12},{3,13},{4,10},{5,11},{0,8},{1,9},{6,14},{7,15},{10,20},{11,... | collective-permute-start | bytes 1769480 | tf_op jit(solution)/shard_map/ppermute | solution.py:41
  126.2 21.8 %collective-permute-start.20 = (bf16[96,3072]{1,0:T(8,128)(2,1)S(1)}, bf16[96,3072]{1,0:T(8,128)(2,1)S(1)}, u32[]{:S(2)}, u32[]{:S(2)}) collective-permute-start(bf16[96,3072]{1,0:T(8,128)(2,1)S(1)} %get-tuple-element.48), channel_id=1, source_target_pairs={{0,2},{1,3},{6,4},{7,5},{8,10},{9,11},{14,12},{15,13},{16,18},{17,... | collective-permute-start | bytes 1769480 | tf_op jit(solution)/shard_map/ppermute | solution.py:25
  138.3 16.6 %collective-permute-start.16 = (bf16[96,3072]{1,0:T(8,128)(2,1)S(1)}, bf16[96,3072]{1,0:T(8,128)(2,1)S(1)}, u32[]{:S(2)}, u32[]{:S(2)}) collective-permute-start(bf16[96,3072]{1,0:T(8,128)(2,1)S(1)} %add_convert_fusion.7), channel_id=1, source_target_pairs={{0,10},{1,11},{2,8},{3,9},{4,14},{5,15},{6,12},{7,13},{8,18},{9,19... | collective-permute-start | bytes 1769480 | tf_op jit(solution)/shard_map/ppermute | solution.py:41
  148.0 1.7 collective-permute-start.23
  149.7 16.6 %collective-permute-start.21 = (bf16[96,3072]{1,0:T(8,128)(2,1)}, bf16[96,3072]{1,0:T(8,128)(2,1)S(1)}, u32[]{:S(2)}, u32[]{:S(2)}) collective-permute-start(bf16[96,3072]{1,0:T(8,128)(2,1)} %fusion), channel_id=1, source_target_pairs={{2,13},{3,12},{4,11},{5,10},{0,9},{1,8},{6,15},{7,14},{10,21},{11,... | collective-permute-start | bytes 1769480 | tf_op jit(solution)/shard_map/ppermute | solution.py:41
  154.9 33.0 %collective-permute-start.24 = (bf16[96,3072]{1,0:T(8,128)(2,1)}, bf16[96,3072]{1,0:T(8,128)(2,1)S(1)}, u32[]{:S(2)}, u32[]{:S(2)}) collective-permute-start(bf16[96,3072]{1,0:T(8,128)(2,1)} %add_convert_fusion.2), channel_id=1, source_target_pairs={{0,11},{1,10},{2,9},{3,8},{4,15},{5,14},{6,13},{7,12},{8,19},{9,18... | collective-permute-start | bytes 1769480 | tf_op jit(solution)/shard_map/ppermute | solution.py:41

commit v2 on v1

v2 whole, which is shorter than its diff:
```python
import functools

import jax
import jax.numpy as jnp
from jax import lax
from jax.experimental import pallas as pl
from jax.experimental.pallas import tpu as pltpu
from jax.sharding import PartitionSpec as P

CORES = 2
VMEM_LIMIT = 14 * 1024 * 1024
CHIPS = 4
BF16 = jnp.bfloat16
F32 = jnp.float32

NEAR = [(0, 1), (1, 0), (2, 3), (3, 2)]
MIDDLE = [(1, 2), (2, 1)]
STAY = [(0, 0), (1, 1), (2, 2), (3, 3)]


def along_line(value, pairs):
    full = [(CORES * a + c, CORES * b + c) for a, b in pairs for c in range(CORES)]
    return lax.ppermute(value, "tensor", full)


def across_cores(value):
    count = lax.axis_size("tensor")
    return lax.ppermute(value, "tensor", [(i, i ^ 1) for i in range(count)])


def to_next_phase(value, pairs, cross):
    segments, count = lax.axis_size("segment"), lax.axis_size("tensor")
    full = [
        (s * count + CORES * a + c, ((s + 1) % segments) * count + CORES * b + (c ^ cross))
        for s in range(segments)
        for a, b in pairs
        for c in range(CORES)
    ]
    return lax.ppermute(value, ("segment", "tensor"), full)


def ffn_kernel(layout, out_rows, *refs):
    n_in = sum(choices for choices, _ in layout)
    n_out = len(out_rows)
    meta, slot_rows, slot_gates = refs[:3]
    x_refs = refs[3 : 3 + n_in]
    weights = refs[3 + n_in : 9 + n_in]
    outs = refs[9 + n_in : 9 + n_in + n_out]
    x, h, gate = refs[9 + n_in + n_out :]
    hidden_units, features = weights[2].shape

    second = meta[0] == 1
    start = at = run = 0
    for choices, runs in layout:
        here = pl.ds(start, sum(runs))
        if choices == 1:
            x[here, :] = x_refs[at][...]
        else:
            first_ref, second_ref = x_refs[at], x_refs[at + 1]

            @pl.when(second)
            def _(here=here, ref=second_ref):
                x[here, :] = ref[...]

            @pl.when(jnp.logical_not(second))
            def _(here=here, ref=first_ref):
                x[here, :] = ref[...]

        at += choices
        for rows in runs:
            tokens = meta[1 + run] + lax.broadcasted_iota(
                jnp.int32, (rows, slot_rows.shape[1]), 0
            )
            named = jnp.where(slot_rows[...] == tokens, slot_gates[...], 0.0)
            column = jnp.sum(named, axis=1, keepdims=True)
            gate[pl.ds(start, rows), :] = jnp.broadcast_to(column, (rows, gate.shape[1]))
            start += rows
            run += 1

    width = 256 if hidden_units % 256 == 0 else hidden_units
    for core in range(CORES):
        for begin in range(0, hidden_units, width):
            g = jnp.dot(x[...], weights[3 * core][:, begin : begin + width], preferred_element_type=F32)
            u = jnp.dot(x[...], weights[3 * core + 1][:, begin : begin + width], preferred_element_type=F32)
            at = core * hidden_units + begin
            h[:, at : at + width] = (g / (1.0 + jnp.exp(-g)) * u).astype(BF16)
    out_width = 768 if features % 768 == 0 else features
    for begin in range(0, features, out_width):
        span = slice(begin, begin + out_width)
        y = jnp.dot(h[:, :hidden_units], weights[2][:, span], preferred_element_type=F32)
        y += jnp.dot(h[:, hidden_units:], weights[5][:, span], preferred_element_type=F32)
        y = (y * gate[:, :1]).astype(BF16)
        start = 0
        for rows, out in zip(out_rows, outs):
            out[:, span] = y[start : start + rows, :]
            start += rows


def ffn(meta, slot_rows, slot_gates, inputs, runs, weights, out_rows):
    layout = tuple((len(choice), rows) for choice, rows in zip(inputs, runs))
    features, hidden_units = weights[0].shape
    total = sum(out_rows)
    vmem = pl.BlockSpec(memory_space=pltpu.VMEM)
    flat = [value for choice in inputs for value in choice]
    return pl.pallas_call(
        functools.partial(ffn_kernel, layout, out_rows),
        out_shape=[jax.ShapeDtypeStruct((rows, features), BF16) for rows in out_rows],
        in_specs=[pl.BlockSpec(memory_space=pltpu.SMEM)] + [vmem] * (8 + len(flat)),
        out_specs=[vmem] * len(out_rows),
        scratch_shapes=[
            pltpu.VMEM((total, features), BF16),
            pltpu.VMEM((total, CORES * hidden_units), BF16),
            pltpu.VMEM((total, 128), F32),
        ],
        compiler_params=pltpu.CompilerParams(vmem_limit_bytes=VMEM_LIMIT),
        cost_estimate=pl.CostEstimate(
            flops=24 * 10**6 * total, bytes_accessed=0, transcendentals=0
        ),
    )(meta, slot_rows, slot_gates, *flat, *weights)


def add(*values):
    return sum(value.astype(F32) for value in values).astype(BF16)


def after(value, *events):
    return lax.optimization_barrier((value, *events))[0]


def staged(hidden, gate_weight, up_weight, down_weight, block_rows, slot_gate, parts):
    rows_here, features = hidden.shape[2], hidden.shape[3]
    slots = block_rows.shape[2] * block_rows.shape[3]
    index = lax.axis_index("tensor")
    core, chip = index % CORES, index // CORES
    right = chip >= CHIPS // 2
    inner = jnp.logical_and(chip > 0, chip < CHIPS - 1).astype(jnp.int32)

    mine = lax.dynamic_index_in_dim(hidden[0], core, 0, keepdims=False)
    theirs = lax.dynamic_index_in_dim(hidden[0], 1 - core, 0, keepdims=False)
    mine = lax.optimization_barrier(mine)
    slot_rows = lax.dynamic_index_in_dim(block_rows[0], core, 0, keepdims=False).reshape(1, slots)
    slot_gates = lax.dynamic_index_in_dim(slot_gate[0], core, 0, keepdims=False).reshape(1, slots)

    chunks = []
    for half, sizes in enumerate(parts):
        start = 0
        for size in sizes:
            chunks.append((half, start, size))
            start += size
    last = len(chunks)

    def meta_of(runs):
        values = [inner]
        for mirrored_block, chunk in runs:
            half, start, _ = chunks[chunk]
            block = jnp.where(right, CHIPS - 1 - mirrored_block, mirrored_block)
            owner = block * CORES + (core if half == 0 else 1 - core)
            values.append(owner * rows_here + start)
        return jnp.stack(values).astype(jnp.int32)

    every, own_block = range(last), [inner, 1 - inner]
    metas = [meta_of([(block, k) for block in own_block for k in every])]
    metas += [meta_of([(2, k), (3, k)]) for k in every]
    low, at_inner = core == 0, inner == 1
    other, own_weights, metas, low, at_inner, slot_rows, slot_gates = lax.optimization_barrier(
        (
            across_cores(theirs),
            [gate_weight[0], up_weight[0], down_weight[0]],
            metas,
            low,
            at_inner,
            slot_rows,
            slot_gates,
        )
    )
    pieces = [
        (mine if half == 0 else other)[start : start + size] for half, start, size in chunks
    ]

    sizes = [size for _, _, size in chunks]

    near = [along_line(pieces[0], NEAR)]
    rest = along_line(jnp.concatenate(pieces[1:], axis=0), NEAR)
    start = 0
    for size in sizes[1:]:
        near.append(rest[start : start + size])
        start += size
    weights = own_weights + [across_cores(weight) for weight in own_weights]

    def expert(meta, inputs, runs, out_rows):
        return list(ffn(meta, slot_rows, slot_gates, inputs, runs, weights, out_rows))

    across = [
        along_line(jnp.concatenate([piece, value], axis=0), MIDDLE)
        for piece, value in zip(pieces, near)
    ]

    def exchange(k):
        if k < 2:
            payload = across[k]
        elif k < last:
            payload = jnp.where(at_inner, across[k], parts_far[k - 2])
        else:
            payload = parts_far[k - 2]
        return along_line(payload, NEAR)

    parts_far, swapped, over = [], [exchange(0)], []
    for k in range(1, last + 2):
        swapped.append(exchange(k))
        j = k - 1
        if j < last:
            events = parts_far[j - 1 : j]
            if j == 1:
                ready = [after(pieces[0], *events)] + pieces[1:] + near
                out = expert(
                    metas[0], [(value,) for value in ready], [[n] for n in sizes * 2], sizes * 2
                )
                own_part, near_part = out[:last], out[last:]
                events = events + own_part[:1]
            if j == last - 1:
                events = events + over[:1]
            rows = (after(swapped[j], *events), across[j])
            parts_far += expert(metas[1 + j], [rows], [[sizes[j]] * 2], [2 * sizes[j]])
        if k >= 2:
            j = k - 2
            total = add(parts_far[j], swapped[k])
            if j + 1 < last:
                total = after(total, parts_far[j + 1])
            if j > 0:
                total = after(total, over[max(j - 2, 0)])
            over.append(along_line(total, MIDDLE))

    handed, sent = [[], []], []
    for k, (half, _, size) in enumerate(chunks):
        for_pair = add(near_part[k], over[k][size:])
        if k > 1:
            for_pair = after(for_pair, sent[k - 2])
        from_pair = along_line(for_pair, NEAR)
        done = add(pieces[k], own_part[k], over[k][:size], from_pair)
        sent.append(to_next_phase(done, STAY, half))
        handed[half].append(sent[k])
    same, cross = (jnp.concatenate(half, axis=0) for half in handed)
    return jnp.stack([jnp.where(low, same, cross), jnp.where(low, cross, same)])[None]


def whole_gather(hidden, gate_weight, up_weight, down_weight, block_rows, slot_gate):
    rows_here = hidden.shape[2]
    slots = block_rows.shape[2] * block_rows.shape[3]
    total_rows = rows_here * lax.axis_size("tensor")
    gathered = lax.all_gather(hidden, "tensor", axis=2, tiled=True)
    results = []
    for micro_batch in range(hidden.shape[1]):
        x = gathered[0, micro_batch]
        slot_rows = block_rows[0, micro_batch].reshape(1, slots)
        slot_gates = slot_gate[0, micro_batch].reshape(1, slots)
        tokens = lax.broadcasted_iota(jnp.int32, (total_rows, 1), 0)
        gate = jnp.sum(jnp.where(slot_rows == tokens, slot_gates, 0.0), axis=1, keepdims=True)
        gate_act = jnp.dot(x, gate_weight[0], preferred_element_type=F32)
        up_act = jnp.dot(x, up_weight[0], preferred_element_type=F32)
        hidden_act = (jax.nn.silu(gate_act) * up_act).astype(BF16)
        part = jnp.dot(hidden_act, down_weight[0], preferred_element_type=F32) * gate
        placed = lax.psum_scatter(
            part.astype(BF16), "tensor", scatter_dimension=0, tiled=True
        )
        results.append(add(hidden[0, micro_batch], placed))
    count = lax.axis_size("segment")
    pairs = [(source, (source + 1) % count) for source in range(count)]
    return lax.ppermute(jnp.stack(results)[None], "segment", pairs)


def per_device(*args):
    rows_here = args[0].shape[2]
    if (
        lax.axis_size("tensor") != CORES * CHIPS
        or args[0].shape[1] != CORES
        or rows_here % 32 != 0
    ):
        return whole_gather(*args)
    return staged(*args, parts=[[rows_here // 2] * 2] * 2)


def solution(mesh):
    return jax.shard_map(
        per_device,
        mesh=mesh,
        in_specs=(
            P("segment", None, "tensor", None),
            P("segment", None, "tensor"),
            P("segment", None, "tensor"),
            P("segment", "tensor", None),
            P("segment", None, None, None),
            P("segment", None, None, None),
        ),
        out_specs=P("segment", None, "tensor", None),
        check_vma=False,
    )
```

time: 191 us -> 167 us (0.87)
  waiting for transfers between devices: 93.4 us -> 66.6 us
  starting transfers between devices: 50.6 us -> 64 us
  Pallas kernels: 31.2 us -> 24.3 us
    ppermute x15 -> x20, starting transfers between devices: 34.9 us -> 57.1 us  [along_line(): return lax.ppermute(value, 'tensor', full)]
    ppermute x15 -> x20, waiting for transfers between devices: 65.5 us -> 47.3 us  [along_line(): return lax.ppermute(value, 'tensor', full)]
    ppermute x6 -> x4, starting transfers between devices: 14.3 us -> 5.76 us  [to_next_phase(): return lax.ppermute(value, ('segment', 'tensor'), full)]
    ppermute x6 -> x4, waiting for transfers between devices: 26.2 us -> 19.3 us  [to_next_phase(): return lax.ppermute(value, ('segment', 'tensor'), full)]
    pallas_call x3 -> x5, Pallas kernels: 31.2 us -> 24.3 us  [ffn(): pl.pallas_call(functools.partial(ffn_kernel, layout, out_rows), out_shape...]
    unnamed x16 -> x14, local copies, waits for them, and re-layouts: 4.61 us -> 0.41 us
    concatenate x0 -> x5, other arithmetic: none -> 2.34 us  [the longest x4 1.21 us: staged(): jnp.concatenate([piece, value], axis=0)]
    slice x0 -> x3, local copies, waits for them, and re-layouts: none -> 2.06 us  [the longest x2 2 us: staged(): (mine if half == 0 else other)[start:start + size]]
  transfers between devices with their start and end apart: 25 -> 28, of which waited for: 11 -> 14; matrix products, arithmetic and copies ran while one was open for 3% -> 4% of each run, Pallas kernels for 16% -> 15%
where the time goes in v2:
time: 167 us
  waiting for transfers between devices  66.6 us (40%)
  starting transfers between devices  64 us (38%)
  Pallas kernels  24.3 us (15%)
  other arithmetic  6.6 us (4%)
  local copies, waits for them, and re-layouts  4.86 us (3%)
    ppermute x20, starting transfers between devices, along_line(): return lax.ppermute(value, 'tensor', full)  57.1 us
    ppermute x20, waiting for transfers between devices, along_line(): return lax.ppermute(value, 'tensor', full)  47.3 us
    pallas_call x5, Pallas kernels, ffn(): pl.pallas_call(functools.partial(ffn_kernel, layout, out_rows), out_shape...  24.3 us
    ppermute x4, waiting for transfers between devices, to_next_phase(): return lax.ppermute(value, ('segment', 'tensor'), full)  19.3 us
    ppermute x4, starting transfers between devices, to_next_phase(): return lax.ppermute(value, ('segment', 'tensor'), full)  5.76 us
  transfers between devices with their start and end apart: 28, of which 14 were waited for; matrix products, arithmetic and copies ran while one was open for 4% of the time, Pallas kernels for 15%

profile of v2, /device:TPU:0, one launch (start us, length us, event | category | flops | bytes accessed | tf_op | source)
XLA Modules:
  0.0 166.7 jit_solution(12442856632772841227)
XLA Ops:
  0.0 2.3 %dynamic-slice_bitcast_fusion = (bf16[96,3072]{1,0:T(8,128)(2,1)S(1)}, bf16[96,3072]{1,0:T(8,128)(2,1)}) fusion(bf16[1,2,96,3072]{3,2,1,0:T(8,128)(2,1)} %param.6, s32[]{:T(128)S(6)} %select_n.90, s32[]{:T(128)S(6)} %select_n.84), kind=kLoop, calls=%fused_computation.20 | loop fusion | bytes 2359304 | tf_op jit(solution)/shard_map/jit(dynamic_index_in_dim)/squeeze | solution.py:138
  2.3 0.5 collective-permute-start
  2.7 0.4 copy-done.4
  3.1 0.8 fusion.2
  3.9 3.0 %collective-permute-start.1 = (bf16[48,3072]{1,0:T(8,128)(2,1)}, bf16[48,3072]{1,0:T(8,128)(2,1)}, u32[]{:S(2)}, u32[]{:S(2)}) collective-permute-start(bf16[48,3072]{1,0:T(8,128)(2,1)} %get-tuple-element.46.refs_3_), channel_id=1, source_target_pairs={{0,2},{1,3},{2,0},{3,1},{4,6},{5,7},{6,4},{7,5},{8,10},{9,11},{10,... | collective-permute-start | bytes 884744 | tf_op jit(solution)/shard_map/ppermute | solution.py:23
  6.9 0.1 stack.84.refs_0_
  7.0 0.1 pad_add_fusion.2
  7.1 0.1 pad_add_fusion
  7.3 0.5 collective-permute-start.5
  7.8 0.1 collective-permute-start.6
  7.9 1.1 pad_maximum_fusion
  9.0 0.5 collective-permute-start.7
  9.5 5.5 %collective-permute-done.1.refs_7_ = bf16[48,3072]{1,0:T(8,128)(2,1)} collective-permute-done((bf16[48,3072]{1,0:T(8,128)(2,1)}, bf16[48,3072]{1,0:T(8,128)(2,1)}, u32[]{:S(2)}, u32[]{:S(2)}) %collective-permute-start.1) | collective-permute-done | bytes 294944 | tf_op jit(solution)/shard_map/ppermute | solution.py:23
  15.1 1.1 pad_maximum_fusion.1
  16.2 0.7 collective-permute-start.2
  16.9 1.2 fusion.1
  18.1 15.0 %collective-permute-start.3 = (bf16[96,3072]{1,0:T(8,128)(2,1)S(1)}, bf16[96,3072]{1,0:T(8,128)(2,1)S(1)}, u32[]{:S(2)}, u32[]{:S(2)}) collective-permute-start(bf16[96,3072]{1,0:T(8,128)(2,1)S(1)} %collective-permute-done.2.refs_4_), channel_id=1, source_target_pairs={{0,2},{1,3},{2,0},{3,1},{4,6},{5,7},{6,4},{7,5},{8,10},{9,11},{10,... | collective-permute-start | bytes 1769480 | tf_op jit(solution)/shard_map/ppermute | solution.py:23
  33.2 0.8 collective-permute-done.7
  34.0 0.8 collective-permute-start.10
  34.9 10.8 %collective-permute-done.3.refs_3_ = bf16[96,3072]{1,0:T(8,128)(2,1)S(1)} collective-permute-done((bf16[96,3072]{1,0:T(8,128)(2,1)S(1)}, bf16[96,3072]{1,0:T(8,128)(2,1)S(1)}, u32[]{:S(2)}, u32[]{:S(2)}) %collective-permute-start.3) | collective-permute-done | bytes 589856 | tf_op jit(solution)/shard_map/ppermute | solution.py:23
  45.7 0.7 collective-permute-start.8
  46.5 0.7 collective-permute-start.15
  47.2 8.8 %collective-permute-start.11 = (bf16[96,3072]{1,0:T(8,128)(2,1)S(1)}, bf16[96,3072]{1,0:T(8,128)(2,1)S(1)}, u32[]{:S(2)}, u32[]{:S(2)}) collective-permute-start(bf16[96,3072]{1,0:T(8,128)(2,1)S(1)} %collective-permute-done.10.refs_4_), channel_id=1, source_target_pairs={{0,2},{1,3},{2,0},{3,1},{4,6},{5,7},{6,4},{7,5},{8,10},{9,11},{10,... | collective-permute-start | bytes 1769480 | tf_op jit(solution)/shard_map/ppermute | solution.py:23
  56.0 3.8 %shard_map.64 = bf16[96,3072]{1,0:T(8,128)(2,1)S(1)} custom-call(s32[3]{0:T(128)S(1)} %get-tuple-element.42.refs_0_, s32[1,768]{1,0:T(1,128)S(1)} %dynamic-slice_bitcast_fusion.3.refs_1_, f32[1,768]{1,0:T(1,128)S(1)} %dynamic-slice_bitcast_fusion.2.refs_2_, bf16[96,3072]{1,0:T(8,128)(2,1)S(1)} %collective-permute-done.3.refs_3_, ...), custom_call_target="tpu_custom_call" | custom-call | flops 2304000000 | tf_op jit(solution)/shard_map/pallas_call | solution.py:105
  59.9 0.1 broadcast_select_fusion.1
  60.0 5.8 %collective-permute-start.9 = (bf16[96,3072]{1,0:T(8,128)(2,1)S(1)}, bf16[96,3072]{1,0:T(8,128)(2,1)S(1)}, u32[]{:S(2)}, u32[]{:S(2)}) collective-permute-start(bf16[96,3072]{1,0:T(8,128)(2,1)S(1)} %broadcast_select_fusion.1), channel_id=1, source_target_pairs={{0,2},{1,3},{2,0},{3,1},{4,6},{5,7},{6,4},{7,5},{8,10},{9,11},{10,... | collective-permute-start | bytes 1769480 | tf_op jit(solution)/shard_map/ppermute | solution.py:23
  65.8 8.7 %shard_map.65 = (bf16[48,3072]{1,0:T(8,128)(2,1)S(1)}, bf16[48,3072]{1,0:T(8,128)(2,1)S(1)}, bf16[48,3072]{1,0:T(8,128)(2,1)S(1)}, bf16[48,3072]{1,0:T(8,128)(2,...) custom-call(s32[9]{0:T(128)S(1)} %stack.84.refs_0_, ...), custom_call_target="tpu_custom_call" | custom-call | flops 9216000000 | tf_op jit(solution)/shard_map/pallas_call | solution.py:105
  74.5 4.0 %shard_map.66 = bf16[96,3072]{1,0:T(8,128)(2,1)S(1)} custom-call(s32[3]{0:T(128)S(1)} %get-tuple-element.50.refs_0_, s32[1,768]{1,0:T(1,128)S(1)} %dynamic-slice_bitcast_fusion.3.refs_1_, f32[1,768]{1,0:T(1,128)S(1)} %dynamic-slice_bitcast_fusion.2.refs_2_, bf16[96,3072]{1,0:T(8,128)(2,1)S(1)} %collective-permute-done.11.refs_3_, ...), custom_call_target="tpu_custom_call" | custom-call | flops 2304000000 | tf_op jit(solution)/shard_map/pallas_call | solution.py:105
  78.6 0.1 broadcast_select_fusion
  78.6 0.1 collective-permute-start.16
  78.8 0.1 add_convert_fusion.3
  78.9 0.7 collective-permute-start.12
  79.6 3.8 %shard_map.67 = bf16[96,3072]{1,0:T(8,128)(2,1)S(1)} custom-call(s32[3]{0:T(128)S(1)} %get-tuple-element.55.refs_0_, s32[1,768]{1,0:T(1,128)S(1)} %dynamic-slice_bitcast_fusion.3.refs_1_, f32[1,768]{1,0:T(1,128)S(1)} %dynamic-slice_bitcast_fusion.2.refs_2_, bf16[96,3072]{1,0:T(8,128)(2,1)S(1)} %collective-permute-done.9.refs_3_, ...), custom_call_target="tpu_custom_call" | custom-call | flops 2304000000 | tf_op jit(solution)/shard_map/pallas_call | solution.py:105
  83.5 4.8 %collective-permute-start.20 = (bf16[96,3072]{1,0:T(8,128)(2,1)S(1)}, bf16[96,3072]{1,0:T(8,128)(2,1)S(1)}, u32[]{:S(2)}, u32[]{:S(2)}) collective-permute-start(bf16[96,3072]{1,0:T(8,128)(2,1)S(1)} %shard_map.67), channel_id=1, source_target_pairs={{0,2},{1,3},{2,0},{3,1},{4,6},{5,7},{6,4},{7,5},{8,10},{9,11},{10,... | collective-permute-start | bytes 1769480 | tf_op jit(solution)/shard_map/ppermute | solution.py:23
  88.3 6.7 %collective-permute-done.16.refs_3_ = bf16[96,3072]{1,0:T(8,128)(2,1)S(1)} collective-permute-done((bf16[96,3072]{1,0:T(8,128)(2,1)S(1)}, bf16[96,3072]{1,0:T(8,128)(2,1)S(1)}, u32[]{:S(2)}, u32[]{:S(2)}) %collective-permute-start.16) | collective-permute-done | bytes 589856 | tf_op jit(solution)/shard_map/ppermute | solution.py:23
  95.0 0.1 add_convert_fusion.2
  95.1 3.8 %shard_map.68 = bf16[96,3072]{1,0:T(8,128)(2,1)S(1)} custom-call(s32[3]{0:T(128)S(1)} %get-tuple-element.61.refs_0_, s32[1,768]{1,0:T(1,128)S(1)} %dynamic-slice_bitcast_fusion.3.refs_1_, f32[1,768]{1,0:T(1,128)S(1)} %dynamic-slice_bitcast_fusion.2.refs_2_, bf16[96,3072]{1,0:T(8,128)(2,1)S(1)} %collective-permute-done.16.refs_3_, ...), custom_call_target="tpu_custom_call" | custom-call | flops 2304000000 | tf_op jit(solution)/shard_map/pallas_call | solution.py:105
  99.0 0.1 collective-permute-start.24
  99.1 0.7 collective-permute-start.17
  99.9 4.8 %collective-permute-start.13 = (bf16[48,3072]{1,0:T(8,128)(2,1)S(1)}, bf16[48,3072]{1,0:T(8,128)(2,1)S(1)}, u32[]{:S(2)}, u32[]{:S(2)}) collective-permute-start(bf16[48,3072]{1,0:T(8,128)(2,1)S(1)} %add_convert_fusion.11), channel_id=1, source_target_pairs={{0,2},{1,3},{2,0},{3,1},{4,6},{5,7},{6,4},{7,5},{8,10},{9,11},{10,... | collective-permute-start | bytes 884744 | tf_op jit(solution)/shard_map/ppermute | solution.py:23
  104.7 2.9 %collective-permute-done.20 = bf16[96,3072]{1,0:T(8,128)(2,1)S(1)} collective-permute-done((bf16[96,3072]{1,0:T(8,128)(2,1)S(1)}, bf16[96,3072]{1,0:T(8,128)(2,1)S(1)}, u32[]{:S(2)}, u32[]{:S(2)}) %collective-permute-start.20) | collective-permute-done | bytes 589856 | tf_op jit(solution)/shard_map/ppermute | solution.py:23
  107.6 0.2 add_convert_fusion.1
  107.8 0.7 collective-permute-start.21
  108.5 11.2 %collective-permute-done.24 = bf16[96,3072]{1,0:T(8,128)(2,1)S(1)} collective-permute-done((bf16[96,3072]{1,0:T(8,128)(2,1)S(1)}, bf16[96,3072]{1,0:T(8,128)(2,1)S(1)}, u32[]{:S(2)}, u32[]{:S(2)}) %collective-permute-start.24) | collective-permute-done | bytes 589856 | tf_op jit(solution)/shard_map/ppermute | solution.py:23
  119.7 0.2 add_convert_fusion
  119.8 0.8 collective-permute-start.25
  120.8 3.5 %collective-permute-start.18 = (bf16[48,3072]{1,0:T(8,128)(2,1)S(1)}, bf16[48,3072]{1,0:T(8,128)(2,1)S(1)}, u32[]{:S(2)}, u32[]{:S(2)}) collective-permute-start(bf16[48,3072]{1,0:T(8,128)(2,1)S(1)} %add_convert_fusion.9), channel_id=1, source_target_pairs={{0,2},{1,3},{2,0},{3,1},{4,6},{5,7},{6,4},{7,5},{8,10},{9,11},{10,... | collective-permute-start | bytes 884744 | tf_op jit(solution)/shard_map/ppermute | solution.py:23
  124.3 0.9 collective-permute-done.13
  125.2 3.8 %collective-permute-done.18 = bf16[48,3072]{1,0:T(8,128)(2,1)S(1)} collective-permute-done((bf16[48,3072]{1,0:T(8,128)(2,1)S(1)}, bf16[48,3072]{1,0:T(8,128)(2,1)S(1)}, u32[]{:S(2)}, u32[]{:S(2)}) %collective-permute-start.18) | collective-permute-done | bytes 294944 | tf_op jit(solution)/shard_map/ppermute | solution.py:23
  129.0 0.3 add_convert_fusion.10
  129.3 1.5 collective-permute-start.19
  130.8 1.5 collective-permute-start.14
  132.4 5.5 %collective-permute-done.19 = bf16[48,3072]{1,0:T(8,128)(2,1)S(1)} collective-permute-done((bf16[48,3072]{1,0:T(8,128)(2,1)S(1)}, bf16[48,3072]{1,0:T(8,128)(2,1)S(1)}, u32[]{:S(2)}, u32[]{:S(2)}) %collective-permute-start.19) | collective-permute-done | bytes 294944 | tf_op jit(solution)/shard_map/ppermute | solution.py:39
  137.9 2.4 %collective-permute-start.26 = (bf16[48,3072]{1,0:T(8,128)(2,1)S(1)}, bf16[48,3072]{1,0:T(8,128)(2,1)S(1)}, u32[]{:S(2)}, u32[]{:S(2)}) collective-permute-start(bf16[48,3072]{1,0:T(8,128)(2,1)S(1)} %add_convert_fusion.5), channel_id=1, source_target_pairs={{0,2},{1,3},{2,0},{3,1},{4,6},{5,7},{6,4},{7,5},{8,10},{9,11},{10,... | collective-permute-start | bytes 884744 | tf_op jit(solution)/shard_map/ppermute | solution.py:23
  140.2 0.8 collective-permute-done.14
  141.0 2.4 %collective-permute-start.22 = (bf16[48,3072]{1,0:T(8,128)(2,1)S(1)}, bf16[48,3072]{1,0:T(8,128)(2,1)S(1)}, u32[]{:S(2)}, u32[]{:S(2)}) collective-permute-start(bf16[48,3072]{1,0:T(8,128)(2,1)S(1)} %add_convert_fusion.7), channel_id=1, source_target_pairs={{0,2},{1,3},{2,0},{3,1},{4,6},{5,7},{6,4},{7,5},{8,10},{9,11},{10,... | collective-permute-start | bytes 884744 | tf_op jit(solution)/shard_map/ppermute | solution.py:23
  143.4 1.6 collective-permute-done.26
  145.0 3.2 %collective-permute-done.22 = bf16[48,3072]{1,0:T(8,128)(2,1)S(1)} collective-permute-done((bf16[48,3072]{1,0:T(8,128)(2,1)S(1)}, bf16[48,3072]{1,0:T(8,128)(2,1)S(1)}, u32[]{:S(2)}, u32[]{:S(2)}) %collective-permute-start.22) | collective-permute-done | bytes 294944 | tf_op jit(solution)/shard_map/ppermute | solution.py:23
  148.1 1.4 add_convert_fusion.6
  149.6 2.7 %collective-permute-start.27 = (bf16[48,3072]{1,0:T(8,128)(2,1)S(1)}, bf16[48,3072]{1,0:T(8,128)(2,1)S(1)}, u32[]{:S(2)}, u32[]{:S(2)}) collective-permute-start(bf16[48,3072]{1,0:T(8,128)(2,1)S(1)} %get-tuple-element.79), channel_id=1, source_target_pairs={{0,9},{1,8},{2,11},{3,10},{4,13},{5,12},{6,15},{7,14},{8,17},{9,16... | collective-permute-start | bytes 884744 | tf_op jit(solution)/shard_map/ppermute | solution.py:39
  152.3 7.5 %collective-permute-done.23 = bf16[48,3072]{1,0:T(8,128)(2,1)S(1)} collective-permute-done((bf16[48,3072]{1,0:T(8,128)(2,1)S(1)}, bf16[48,3072]{1,0:T(8,128)(2,1)S(1)}, u32[]{:S(2)}, u32[]{:S(2)}) %collective-permute-start.23) | collective-permute-done | bytes 294944 | tf_op jit(solution)/shard_map/ppermute | solution.py:39
  159.8 5.5 %collective-permute-done.27 = bf16[48,3072]{1,0:T(8,128)(2,1)S(1)} collective-permute-done((bf16[48,3072]{1,0:T(8,128)(2,1)S(1)}, bf16[48,3072]{1,0:T(8,128)(2,1)S(1)}, u32[]{:S(2)}, u32[]{:S(2)}) %collective-permute-start.27) | collective-permute-done | bytes 294944 | tf_op jit(solution)/shard_map/ppermute | solution.py:39
  165.3 0.2 broadcast_select_fusion.3
  165.5 1.1 maximum_bitcast_fusion
  (39 shorter events, 0.7 us)
Async XLA Ops:
  0.0 7.2 %copy-start = (f32[1,2,6,128]{3,1,2,0:T(2,128)S(1)}, f32[1,2,6,128]{3,1,2,0:T(2,128)}, u32[]{:S(2)}) copy-start(f32[1,2,6,128]{3,1,2,0:T(2,128)} %param.11) | copy-start | bytes 18436
  0.0 7.2 %copy-start.1 = (bf16[1,3072,512]{2,1,0:T(8,128)(2,1)S(1)}, bf16[1,3072,512]{2,1,0:T(8,128)(2,1)}, u32[]{:S(2)}) copy-start(bf16[1,3072,512]{2,1,0:T(8,128)(2,1)} %param.7) | copy-start | bytes 9437188
  2.3 0.8 copy-start.4
  2.3 4.9 %copy-start.6 = (s32[1,2,6,128]{3,1,2,0:T(2,128)S(1)}, s32[1,2,6,128]{3,1,2,0:T(2,128)}, u32[]{:S(2)}) copy-start(s32[1,2,6,128]{3,1,2,0:T(2,128)} %param.10) | copy-start | bytes 18436
  2.3 4.9 %collective-permute-start = (bf16[96,3072]{1,0:T(8,128)(2,1)}, bf16[96,3072]{1,0:T(8,128)(2,1)}, u32[]{:S(2)}, u32[]{:S(2)}) collective-permute-start(bf16[96,3072]{1,0:T(8,128)(2,1)} %get-tuple-element.74), channel_id=1, source_target_pairs={{0,1},{1,0},{2,3},{3,2},{4,5},{5,4},{6,7},{7,6},{8,9},{9,8},{10,11... | collective-permute-start | bytes 1769480 | tf_op jit(solution)/shard_map/ppermute | solution.py:28
  3.9 11.2 %collective-permute-start.1 = (bf16[48,3072]{1,0:T(8,128)(2,1)}, bf16[48,3072]{1,0:T(8,128)(2,1)}, u32[]{:S(2)}, u32[]{:S(2)}) collective-permute-start(bf16[48,3072]{1,0:T(8,128)(2,1)} %get-tuple-element.46.refs_3_), channel_id=1, source_target_pairs={{0,2},{1,3},{2,0},{3,1},{4,6},{5,7},{6,4},{7,5},{8,10},{9,11},{10,... | collective-permute-start | bytes 884744 | tf_op jit(solution)/shard_map/ppermute | solution.py:23
  7.2 40.0 %collective-permute-start.4 = (bf16[3072,512]{1,0:T(8,128)(2,1)S(1)}, bf16[3072,512]{1,0:T(8,128)(2,1)S(1)}, u32[]{:S(2)}, u32[]{:S(2)}) collective-permute-start(bf16[3072,512]{1,0:T(8,128)(2,1)S(1)} %bitcast.34), channel_id=1, source_target_pairs={{0,1},{1,0},{2,3},{3,2},{4,5},{5,4},{6,7},{7,6},{8,9},{9,8},{10,11... | collective-permute-start | bytes 9437192 | tf_op jit(solution)/shard_map/ppermute | solution.py:28
  7.3 48.7 %collective-permute-start.5 = (bf16[3072,512]{1,0:T(8,128)(2,1)}, bf16[3072,512]{1,0:T(8,128)(2,1)S(1)}, u32[]{:S(2)}, u32[]{:S(2)}) collective-permute-start(bf16[3072,512]{1,0:T(8,128)(2,1)} %bitcast.40), channel_id=1, source_target_pairs={{0,1},{1,0},{2,3},{3,2},{4,5},{5,4},{6,7},{7,6},{8,9},{9,8},{10,11... | collective-permute-start | bytes 9437192 | tf_op jit(solution)/shard_map/ppermute | solution.py:28
  7.8 48.2 %collective-permute-start.6 = (bf16[512,3072]{1,0:T(8,128)(2,1)}, bf16[512,3072]{1,0:T(8,128)(2,1)S(1)}, u32[]{:S(2)}, u32[]{:S(2)}) collective-permute-start(bf16[512,3072]{1,0:T(8,128)(2,1)} %bitcast.46), channel_id=1, source_target_pairs={{0,1},{1,0},{2,3},{3,2},{4,5},{5,4},{6,7},{7,6},{8,9},{9,8},{10,11... | collective-permute-start | bytes 9437192 | tf_op jit(solution)/shard_map/ppermute | solution.py:28
  9.0 24.9 %collective-permute-start.7 = (bf16[144,3072]{1,0:T(8,128)(2,1)S(1)}, bf16[144,3072]{1,0:T(8,128)(2,1)S(1)}, u32[]{:S(2)}, u32[]{:S(2)}) collective-permute-start(bf16[144,3072]{1,0:T(8,128)(2,1)S(1)} %pad_maximum_fusion), channel_id=1, source_target_pairs={{0,2},{1,3},{2,0},{3,1},{4,6},{5,7},{6,4},{7,5},{8,10},{9,11},{10,... | collective-permute-start | bytes 2654216 | tf_op jit(solution)/shard_map/ppermute | solution.py:23
  16.2 2.0 %collective-permute-start.2 = (bf16[96,3072]{1,0:T(8,128)(2,1)S(1)}, bf16[96,3072]{1,0:T(8,128)(2,1)S(1)}, u32[]{:S(2)}, u32[]{:S(2)}) collective-permute-start(bf16[96,3072]{1,0:T(8,128)(2,1)S(1)} %pad_maximum_fusion.1), channel_id=1, source_target_pairs={{2,4},{3,5},{4,2},{5,3},{10,12},{11,13},{12,10},{13,11},{18,20},{1... | collective-permute-start | bytes 1769480 | tf_op jit(solution)/shard_map/ppermute | solution.py:23
  16.9 39.2 %copy-start.3 = (bf16[1,512,3072]{2,1,0:T(8,128)(2,1)S(1)}, bf16[1,512,3072]{2,1,0:T(8,128)(2,1)}, u32[]{:S(2)}) copy-start(bf16[1,512,3072]{2,1,0:T(8,128)(2,1)} %param.9) | copy-start | bytes 9437188
  18.1 27.6 %collective-permute-start.3 = (bf16[96,3072]{1,0:T(8,128)(2,1)S(1)}, bf16[96,3072]{1,0:T(8,128)(2,1)S(1)}, u32[]{:S(2)}, u32[]{:S(2)}) collective-permute-start(bf16[96,3072]{1,0:T(8,128)(2,1)S(1)} %collective-permute-done.2.refs_4_), channel_id=1, source_target_pairs={{0,2},{1,3},{2,0},{3,1},{4,6},{5,7},{6,4},{7,5},{8,10},{9,11},{10,... | collective-permute-start | bytes 1769480 | tf_op jit(solution)/shard_map/ppermute | solution.py:23
  34.0 22.0 %copy-start.2 = (bf16[1,3072,512]{2,1,0:T(8,128)(2,1)S(1)}, bf16[1,3072,512]{2,1,0:T(8,128)(2,1)}, u32[]{:S(2)}) copy-start(bf16[1,3072,512]{2,1,0:T(8,128)(2,1)} %param.8) | copy-start | bytes 9437188
  34.0 12.4 %collective-permute-start.10 = (bf16[96,3072]{1,0:T(8,128)(2,1)S(1)}, bf16[96,3072]{1,0:T(8,128)(2,1)S(1)}, u32[]{:S(2)}, u32[]{:S(2)}) collective-permute-start(bf16[96,3072]{1,0:T(8,128)(2,1)S(1)} %pad_maximum_fusion.3), channel_id=1, source_target_pairs={{2,4},{3,5},{4,2},{5,3},{10,12},{11,13},{12,10},{13,11},{18,20},{1... | collective-permute-start | bytes 1769480 | tf_op jit(solution)/shard_map/ppermute | solution.py:23
  45.7 14.2 %collective-permute-start.8 = (bf16[96,3072]{1,0:T(8,128)(2,1)S(1)}, bf16[96,3072]{1,0:T(8,128)(2,1)S(1)}, u32[]{:S(2)}, u32[]{:S(2)}) collective-permute-start(bf16[96,3072]{1,0:T(8,128)(2,1)S(1)} %pad_maximum_fusion.2), channel_id=1, source_target_pairs={{2,4},{3,5},{4,2},{5,3},{10,12},{11,13},{12,10},{13,11},{18,20},{1... | collective-permute-start | bytes 1769480 | tf_op jit(solution)/shard_map/ppermute | solution.py:23
  46.5 32.1 %collective-permute-start.15 = (bf16[96,3072]{1,0:T(8,128)(2,1)S(1)}, bf16[96,3072]{1,0:T(8,128)(2,1)S(1)}, u32[]{:S(2)}, u32[]{:S(2)}) collective-permute-start(bf16[96,3072]{1,0:T(8,128)(2,1)S(1)} %pad_maximum_fusion.4), channel_id=1, source_target_pairs={{2,4},{3,5},{4,2},{5,3},{10,12},{11,13},{12,10},{13,11},{18,20},{1... | collective-permute-start | bytes 1769480 | tf_op jit(solution)/shard_map/ppermute | solution.py:23
  47.2 27.3 %collective-permute-start.11 = (bf16[96,3072]{1,0:T(8,128)(2,1)S(1)}, bf16[96,3072]{1,0:T(8,128)(2,1)S(1)}, u32[]{:S(2)}, u32[]{:S(2)}) collective-permute-start(bf16[96,3072]{1,0:T(8,128)(2,1)S(1)} %collective-permute-done.10.refs_4_), channel_id=1, source_target_pairs={{0,2},{1,3},{2,0},{3,1},{4,6},{5,7},{6,4},{7,5},{8,10},{9,11},{10,... | collective-permute-start | bytes 1769480 | tf_op jit(solution)/shard_map/ppermute | solution.py:23
  60.0 18.8 %collective-permute-start.9 = (bf16[96,3072]{1,0:T(8,128)(2,1)S(1)}, bf16[96,3072]{1,0:T(8,128)(2,1)S(1)}, u32[]{:S(2)}, u32[]{:S(2)}) collective-permute-start(bf16[96,3072]{1,0:T(8,128)(2,1)S(1)} %broadcast_select_fusion.1), channel_id=1, source_target_pairs={{0,2},{1,3},{2,0},{3,1},{4,6},{5,7},{6,4},{7,5},{8,10},{9,11},{10,... | collective-permute-start | bytes 1769480 | tf_op jit(solution)/shard_map/ppermute | solution.py:23
  78.6 16.3 %collective-permute-start.16 = (bf16[96,3072]{1,0:T(8,128)(2,1)S(1)}, bf16[96,3072]{1,0:T(8,128)(2,1)S(1)}, u32[]{:S(2)}, u32[]{:S(2)}) collective-permute-start(bf16[96,3072]{1,0:T(8,128)(2,1)S(1)} %broadcast_select_fusion), channel_id=1, source_target_pairs={{0,2},{1,3},{2,0},{3,1},{4,6},{5,7},{6,4},{7,5},{8,10},{9,11},{10,... | collective-permute-start | bytes 1769480 | tf_op jit(solution)/shard_map/ppermute | solution.py:23
  78.9 16.2 %collective-permute-start.12 = (bf16[96,3072]{1,0:T(8,128)(2,1)S(1)}, bf16[96,3072]{1,0:T(8,128)(2,1)S(1)}, u32[]{:S(2)}, u32[]{:S(2)}) collective-permute-start(bf16[96,3072]{1,0:T(8,128)(2,1)S(1)} %add_convert_fusion.3), channel_id=1, source_target_pairs={{2,4},{3,5},{4,2},{5,3},{10,12},{11,13},{12,10},{13,11},{18,20},{1... | collective-permute-start | bytes 1769480 | tf_op jit(solution)/shard_map/ppermute | solution.py:23
  83.5 24.2 %collective-permute-start.20 = (bf16[96,3072]{1,0:T(8,128)(2,1)S(1)}, bf16[96,3072]{1,0:T(8,128)(2,1)S(1)}, u32[]{:S(2)}, u32[]{:S(2)}) collective-permute-start(bf16[96,3072]{1,0:T(8,128)(2,1)S(1)} %shard_map.67), channel_id=1, source_target_pairs={{0,2},{1,3},{2,0},{3,1},{4,6},{5,7},{6,4},{7,5},{8,10},{9,11},{10,... | collective-permute-start | bytes 1769480 | tf_op jit(solution)/shard_map/ppermute | solution.py:23
  99.0 20.7 %collective-permute-start.24 = (bf16[96,3072]{1,0:T(8,128)(2,1)S(1)}, bf16[96,3072]{1,0:T(8,128)(2,1)S(1)}, u32[]{:S(2)}, u32[]{:S(2)}) collective-permute-start(bf16[96,3072]{1,0:T(8,128)(2,1)S(1)} %shard_map.68), channel_id=1, source_target_pairs={{0,2},{1,3},{2,0},{3,1},{4,6},{5,7},{6,4},{7,5},{8,10},{9,11},{10,... | collective-permute-start | bytes 1769480 | tf_op jit(solution)/shard_map/ppermute | solution.py:23
  99.1 20.7 %collective-permute-start.17 = (bf16[96,3072]{1,0:T(8,128)(2,1)S(1)}, bf16[96,3072]{1,0:T(8,128)(2,1)S(1)}, u32[]{:S(2)}, u32[]{:S(2)}) collective-permute-start(bf16[96,3072]{1,0:T(8,128)(2,1)S(1)} %add_convert_fusion.2), channel_id=1, source_target_pairs={{2,4},{3,5},{4,2},{5,3},{10,12},{11,13},{12,10},{13,11},{18,20},{1... | collective-permute-start | bytes 1769480 | tf_op jit(solution)/shard_map/ppermute | solution.py:23
  99.9 25.3 %collective-permute-start.13 = (bf16[48,3072]{1,0:T(8,128)(2,1)S(1)}, bf16[48,3072]{1,0:T(8,128)(2,1)S(1)}, u32[]{:S(2)}, u32[]{:S(2)}) collective-permute-start(bf16[48,3072]{1,0:T(8,128)(2,1)S(1)} %add_convert_fusion.11), channel_id=1, source_target_pairs={{0,2},{1,3},{2,0},{3,1},{4,6},{5,7},{6,4},{7,5},{8,10},{9,11},{10,... | collective-permute-start | bytes 884744 | tf_op jit(solution)/shard_map/ppermute | solution.py:23
  107.8 16.5 %collective-permute-start.21 = (bf16[96,3072]{1,0:T(8,128)(2,1)S(1)}, bf16[96,3072]{1,0:T(8,128)(2,1)S(1)}, u32[]{:S(2)}, u32[]{:S(2)}) collective-permute-start(bf16[96,3072]{1,0:T(8,128)(2,1)S(1)} %add_convert_fusion.1), channel_id=1, source_target_pairs={{2,4},{3,5},{4,2},{5,3},{10,12},{11,13},{12,10},{13,11},{18,20},{1... | collective-permute-start | bytes 1769480 | tf_op jit(solution)/shard_map/ppermute | solution.py:23
  119.8 9.1 %copy-start.5 = (bf16[96,3072]{1,0:T(8,128)(2,1)S(1)}, bf16[96,3072]{1,0:T(8,128)(2,1)}, u32[]{:S(2)}) copy-start(bf16[96,3072]{1,0:T(8,128)(2,1)} %copy-done.4) | copy-start | bytes 1769476
  119.8 12.5 %collective-permute-start.25 = (bf16[96,3072]{1,0:T(8,128)(2,1)S(1)}, bf16[96,3072]{1,0:T(8,128)(2,1)S(1)}, u32[]{:S(2)}, u32[]{:S(2)}) collective-permute-start(bf16[96,3072]{1,0:T(8,128)(2,1)S(1)} %add_convert_fusion), channel_id=1, source_target_pairs={{2,4},{3,5},{4,2},{5,3},{10,12},{11,13},{12,10},{13,11},{18,20},{1... | collective-permute-start | bytes 1769480 | tf_op jit(solution)/shard_map/ppermute | solution.py:23
  120.8 8.2 %collective-permute-start.18 = (bf16[48,3072]{1,0:T(8,128)(2,1)S(1)}, bf16[48,3072]{1,0:T(8,128)(2,1)S(1)}, u32[]{:S(2)}, u32[]{:S(2)}) collective-permute-start(bf16[48,3072]{1,0:T(8,128)(2,1)S(1)} %add_convert_fusion.9), channel_id=1, source_target_pairs={{0,2},{1,3},{2,0},{3,1},{4,6},{5,7},{6,4},{7,5},{8,10},{9,11},{10,... | collective-permute-start | bytes 884744 | tf_op jit(solution)/shard_map/ppermute | solution.py:23
  129.3 8.6 %collective-permute-start.19 = (bf16[48,3072]{1,0:T(8,128)(2,1)S(1)}, bf16[48,3072]{1,0:T(8,128)(2,1)S(1)}, u32[]{:S(2)}, u32[]{:S(2)}) collective-permute-start(bf16[48,3072]{1,0:T(8,128)(2,1)S(1)} %get-tuple-element.81), channel_id=1, source_target_pairs={{0,8},{1,9},{2,10},{3,11},{4,12},{5,13},{6,14},{7,15},{8,16},{9,17... | collective-permute-start | bytes 884744 | tf_op jit(solution)/shard_map/ppermute | solution.py:39
  130.8 10.2 %collective-permute-start.14 = (bf16[48,3072]{1,0:T(8,128)(2,1)S(1)}, bf16[48,3072]{1,0:T(8,128)(2,1)S(1)}, u32[]{:S(2)}, u32[]{:S(2)}) collective-permute-start(bf16[48,3072]{1,0:T(8,128)(2,1)S(1)} %get-tuple-element.80), channel_id=1, source_target_pairs={{0,8},{1,9},{2,10},{3,11},{4,12},{5,13},{6,14},{7,15},{8,16},{9,17... | collective-permute-start | bytes 884744 | tf_op jit(solution)/shard_map/ppermute | solution.py:39
  137.9 7.1 %collective-permute-start.26 = (bf16[48,3072]{1,0:T(8,128)(2,1)S(1)}, bf16[48,3072]{1,0:T(8,128)(2,1)S(1)}, u32[]{:S(2)}, u32[]{:S(2)}) collective-permute-start(bf16[48,3072]{1,0:T(8,128)(2,1)S(1)} %add_convert_fusion.5), channel_id=1, source_target_pairs={{0,2},{1,3},{2,0},{3,1},{4,6},{5,7},{6,4},{7,5},{8,10},{9,11},{10,... | collective-permute-start | bytes 884744 | tf_op jit(solution)/shard_map/ppermute | solution.py:23
  141.0 7.1 %collective-permute-start.22 = (bf16[48,3072]{1,0:T(8,128)(2,1)S(1)}, bf16[48,3072]{1,0:T(8,128)(2,1)S(1)}, u32[]{:S(2)}, u32[]{:S(2)}) collective-permute-start(bf16[48,3072]{1,0:T(8,128)(2,1)S(1)} %add_convert_fusion.7), channel_id=1, source_target_pairs={{0,2},{1,3},{2,0},{3,1},{4,6},{5,7},{6,4},{7,5},{8,10},{9,11},{10,... | collective-permute-start | bytes 884744 | tf_op jit(solution)/shard_map/ppermute | solution.py:23
  149.5 10.2 %collective-permute-start.23 = (bf16[48,3072]{1,0:T(8,128)(2,1)S(1)}, bf16[48,3072]{1,0:T(8,128)(2,1)S(1)}, u32[]{:S(2)}, u32[]{:S(2)}) collective-permute-start(bf16[48,3072]{1,0:T(8,128)(2,1)S(1)} %get-tuple-element.78), channel_id=1, source_target_pairs={{0,9},{1,8},{2,11},{3,10},{4,13},{5,12},{6,15},{7,14},{8,17},{9,16... | collective-permute-start | bytes 884744 | tf_op jit(solution)/shard_map/ppermute | solution.py:39
  149.6 15.7 %collective-permute-start.27 = (bf16[48,3072]{1,0:T(8,128)(2,1)S(1)}, bf16[48,3072]{1,0:T(8,128)(2,1)S(1)}, u32[]{:S(2)}, u32[]{:S(2)}) collective-permute-start(bf16[48,3072]{1,0:T(8,128)(2,1)S(1)} %get-tuple-element.79), channel_id=1, source_target_pairs={{0,9},{1,8},{2,11},{3,10},{4,13},{5,12},{6,15},{7,14},{8,17},{9,16... | collective-permute-start | bytes 884744 | tf_op jit(solution)/shard_map/ppermute | solution.py:39

commit v3 on v2

--- a/solution.py
+++ b/solution.py
@@ -21,6 +21,12 @@
 def along_line(value, pairs):
     full = [(CORES * a + c, CORES * b + c) for a, b in pairs for c in range(CORES)]
     return lax.ppermute(value, "tensor", full)
+
+
+def across_middle(value):
+    inside = [(CORES * a + c, CORES * b + c) for a, b in MIDDLE for c in range(CORES)]
+    ends = [(CORES * a + c, CORES * a + 1 - c) for a in (0, CHIPS - 1) for c in range(CORES)]
+    return lax.ppermute(value, "tensor", inside + ends)
 
 
 def across_cores(value):
@@ -191,7 +197,7 @@
         return list(ffn(meta, slot_rows, slot_gates, inputs, runs, weights, out_rows))
 
     across = [
-        along_line(jnp.concatenate([piece, value], axis=0), MIDDLE)
+        across_middle(jnp.concatenate([piece, value], axis=0))
         for piece, value in zip(pieces, near)
     ]
 
@@ -228,15 +234,17 @@
                 total = after(total, parts_far[j + 1])
             if j > 0:
                 total = after(total, over[max(j - 2, 0)])
-            over.append(along_line(total, MIDDLE))
+            over.append(jnp.where(at_inner, across_middle(total), 0))
 
     handed, sent = [[], []], []
     for k, (half, _, size) in enumerate(chunks):
         for_pair = add(near_part[k], over[k][size:])
-        if k > 1:
-            for_pair = after(for_pair, sent[k - 2])
+        if k == last - 1:
+            for_pair = after(for_pair, sent[0])
         from_pair = along_line(for_pair, NEAR)
         done = add(pieces[k], own_part[k], over[k][:size], from_pair)
+        if k == last - 1:
+            done = after(done, sent[1])
         sent.append(to_next_phase(done, STAY, half))
         handed[half].append(sent[k])
     same, cross = (jnp.concatenate(half, axis=0) for half in handed)

time: 167 us -> 160 us (0.958)
  starting transfers between devices: 64 us -> 50 us
  waiting for transfers between devices: 66.6 us -> 73.3 us
    ppermute x20 -> x12, starting transfers between devices: 57.1 us -> 43.1 us  [along_line(): return lax.ppermute(value, 'tensor', full)]
    ppermute x20 -> x12, waiting for transfers between devices: 47.3 us -> 52.6 us  [along_line(): return lax.ppermute(value, 'tensor', full)]
  transfers between devices with their start and end apart: 28 -> 28, of which waited for: 14 -> 13; matrix products, arithmetic and copies ran while one was open for 4% -> 5% of each run, Pallas kernels for 15% -> 15%
where the time goes in v3:
time: 160 us
  waiting for transfers between devices  73.3 us (46%)
  starting transfers between devices  50 us (31%)
  Pallas kernels  24.3 us (15%)
  other arithmetic  6.76 us (4%)
  local copies, waits for them, and re-layouts  4.86 us (3%)
    ppermute x12, waiting for transfers between devices, along_line(): return lax.ppermute(value, 'tensor', full)  52.6 us
    ppermute x12, starting transfers between devices, along_line(): return lax.ppermute(value, 'tensor', full)  43.1 us
    pallas_call x5, Pallas kernels, ffn(): pl.pallas_call(functools.partial(ffn_kernel, layout, out_rows), out_shape...  24.3 us
    ppermute x4, waiting for transfers between devices, to_next_phase(): return lax.ppermute(value, ('segment', 'tensor'), full)  19.1 us
    ppermute x4, starting transfers between devices, to_next_phase(): return lax.ppermute(value, ('segment', 'tensor'), full)  4.87 us
  transfers between devices with their start and end apart: 28, of which 13 were waited for; matrix products, arithmetic and copies ran while one was open for 5% of the time, Pallas kernels for 15%

profile of v3, /device:TPU:0, one launch (start us, length us, event | category | flops | bytes accessed | tf_op | source)
XLA Modules:
  0.0 159.7 jit_solution(18041679444173860325)
XLA Ops:
  0.0 2.3 %dynamic-slice_bitcast_fusion = (bf16[96,3072]{1,0:T(8,128)(2,1)S(1)}, bf16[96,3072]{1,0:T(8,128)(2,1)}) fusion(bf16[1,2,96,3072]{3,2,1,0:T(8,128)(2,1)} %param.6, s32[]{:T(128)S(6)} %select_n.108, s32[]{:T(128)S(6)} %select_n.102), kind=kLoop, calls=%fused_computation.20 | loop fusion | bytes 2359304 | tf_op jit(solution)/shard_map/jit(dynamic_index_in_dim)/squeeze | solution.py:144
  2.3 0.5 collective-permute-start
  2.7 0.4 copy-done.4
  3.1 0.8 fusion.2
  3.9 3.0 %collective-permute-start.1 = (bf16[48,3072]{1,0:T(8,128)(2,1)}, bf16[48,3072]{1,0:T(8,128)(2,1)}, u32[]{:S(2)}, u32[]{:S(2)}) collective-permute-start(bf16[48,3072]{1,0:T(8,128)(2,1)} %get-tuple-element.46.refs_3_), channel_id=1, source_target_pairs={{0,2},{1,3},{2,0},{3,1},{4,6},{5,7},{6,4},{7,5},{8,10},{9,11},{10,... | collective-permute-start | bytes 884744 | tf_op jit(solution)/shard_map/ppermute | solution.py:23
  6.9 0.1 stack.84.refs_0_
  7.0 0.1 pad_add_fusion.2
  7.1 0.1 pad_add_fusion
  7.2 0.1 collective-permute-start.4
  7.3 0.5 collective-permute-start.5
  7.8 0.1 collective-permute-start.6
  7.9 1.1 pad_maximum_fusion
  9.0 0.5 collective-permute-start.7
  9.5 5.5 %collective-permute-done.1.refs_7_ = bf16[48,3072]{1,0:T(8,128)(2,1)} collective-permute-done((bf16[48,3072]{1,0:T(8,128)(2,1)}, bf16[48,3072]{1,0:T(8,128)(2,1)}, u32[]{:S(2)}, u32[]{:S(2)}) %collective-permute-start.1) | collective-permute-done | bytes 294944 | tf_op jit(solution)/shard_map/ppermute | solution.py:23
  15.1 1.1 pad_maximum_fusion.1
  16.2 0.1 collective-permute-start.2
  16.2 1.2 fusion.1
  17.5 1.6 %collective-permute-done.2.refs_4_ = bf16[96,3072]{1,0:T(8,128)(2,1)S(1)} collective-permute-done((bf16[96,3072]{1,0:T(8,128)(2,1)S(1)}, bf16[96,3072]{1,0:T(8,128)(2,1)S(1)}, u32[]{:S(2)}, u32[]{:S(2)}) %collective-permute-start.2) | collective-permute-done | bytes 589856 | tf_op jit(solution)/shard_map/ppermute | solution.py:29
  19.1 12.2 %collective-permute-start.3 = (bf16[96,3072]{1,0:T(8,128)(2,1)S(1)}, bf16[96,3072]{1,0:T(8,128)(2,1)S(1)}, u32[]{:S(2)}, u32[]{:S(2)}) collective-permute-start(bf16[96,3072]{1,0:T(8,128)(2,1)S(1)} %collective-permute-done.2.refs_4_), channel_id=1, source_target_pairs={{0,2},{1,3},{2,0},{3,1},{4,6},{5,7},{6,4},{7,5},{8,10},{9,11},{10,... | collective-permute-start | bytes 1769480 | tf_op jit(solution)/shard_map/ppermute | solution.py:23
  31.3 2.6 %collective-permute-done.7 = bf16[144,3072]{1,0:T(8,128)(2,1)S(1)} collective-permute-done((bf16[144,3072]{1,0:T(8,128)(2,1)S(1)}, bf16[144,3072]{1,0:T(8,128)(2,1)S(1)}, u32[]{:S(2)}, u32[]{:S(2)}) %collective-permute-start.7) | collective-permute-done | bytes 884768 | tf_op jit(solution)/shard_map/ppermute | solution.py:23
  34.0 0.1 collective-permute-start.10
  34.2 11.6 %collective-permute-done.3.refs_3_ = bf16[96,3072]{1,0:T(8,128)(2,1)S(1)} collective-permute-done((bf16[96,3072]{1,0:T(8,128)(2,1)S(1)}, bf16[96,3072]{1,0:T(8,128)(2,1)S(1)}, u32[]{:S(2)}, u32[]{:S(2)}) %collective-permute-start.3) | collective-permute-done | bytes 589856 | tf_op jit(solution)/shard_map/ppermute | solution.py:23
  45.8 0.6 collective-permute-start.15
  46.4 4.6 %collective-permute-start.11 = (bf16[96,3072]{1,0:T(8,128)(2,1)S(1)}, bf16[96,3072]{1,0:T(8,128)(2,1)S(1)}, u32[]{:S(2)}, u32[]{:S(2)}) collective-permute-start(bf16[96,3072]{1,0:T(8,128)(2,1)S(1)} %collective-permute-done.10.refs_4_), channel_id=1, source_target_pairs={{0,2},{1,3},{2,0},{3,1},{4,6},{5,7},{6,4},{7,5},{8,10},{9,11},{10,... | collective-permute-start | bytes 1769480 | tf_op jit(solution)/shard_map/ppermute | solution.py:23
  50.9 3.8 %shard_map.64 = bf16[96,3072]{1,0:T(8,128)(2,1)S(1)} custom-call(s32[3]{0:T(128)S(1)} %get-tuple-element.42.refs_0_, s32[1,768]{1,0:T(1,128)S(1)} %dynamic-slice_bitcast_fusion.3.refs_1_, f32[1,768]{1,0:T(1,128)S(1)} %dynamic-slice_bitcast_fusion.2.refs_2_, bf16[96,3072]{1,0:T(8,128)(2,1)S(1)} %collective-permute-done.3.refs_3_, ...), custom_call_target="tpu_custom_call" | custom-call | flops 2304000000 | tf_op jit(solution)/shard_map/pallas_call | solution.py:111
  54.8 0.1 broadcast_select_fusion.5
  54.9 9.0 %collective-permute-start.9 = (bf16[96,3072]{1,0:T(8,128)(2,1)S(1)}, bf16[96,3072]{1,0:T(8,128)(2,1)S(1)}, u32[]{:S(2)}, u32[]{:S(2)}) collective-permute-start(bf16[96,3072]{1,0:T(8,128)(2,1)S(1)} %broadcast_select_fusion.5), channel_id=1, source_target_pairs={{0,2},{1,3},{2,0},{3,1},{4,6},{5,7},{6,4},{7,5},{8,10},{9,11},{10,... | collective-permute-start | bytes 1769480 | tf_op jit(solution)/shard_map/ppermute | solution.py:23
  63.9 8.7 %shard_map.65 = (bf16[48,3072]{1,0:T(8,128)(2,1)S(1)}, bf16[48,3072]{1,0:T(8,128)(2,1)S(1)}, bf16[48,3072]{1,0:T(8,128)(2,1)S(1)}, bf16[48,3072]{1,0:T(8,128)(2,...) custom-call(s32[9]{0:T(128)S(1)} %stack.84.refs_0_, ...), custom_call_target="tpu_custom_call" | custom-call | flops 9216000000 | tf_op jit(solution)/shard_map/pallas_call | solution.py:111
  72.7 4.0 %shard_map.66 = bf16[96,3072]{1,0:T(8,128)(2,1)S(1)} custom-call(s32[3]{0:T(128)S(1)} %get-tuple-element.50.refs_0_, s32[1,768]{1,0:T(1,128)S(1)} %dynamic-slice_bitcast_fusion.3.refs_1_, f32[1,768]{1,0:T(1,128)S(1)} %dynamic-slice_bitcast_fusion.2.refs_2_, bf16[96,3072]{1,0:T(8,128)(2,1)S(1)} %collective-permute-done.11.refs_3_, ...), custom_call_target="tpu_custom_call" | custom-call | flops 2304000000 | tf_op jit(solution)/shard_map/pallas_call | solution.py:111
  76.8 0.1 collective-permute-start.16
  76.9 0.1 add_convert_fusion.3
  77.0 0.1 collective-permute-start.12
  77.1 3.8 %shard_map.67 = bf16[96,3072]{1,0:T(8,128)(2,1)S(1)} custom-call(s32[3]{0:T(128)S(1)} %get-tuple-element.55.refs_0_, s32[1,768]{1,0:T(1,128)S(1)} %dynamic-slice_bitcast_fusion.3.refs_1_, f32[1,768]{1,0:T(1,128)S(1)} %dynamic-slice_bitcast_fusion.2.refs_2_, bf16[96,3072]{1,0:T(8,128)(2,1)S(1)} %collective-permute-done.9.refs_3_, ...), custom_call_target="tpu_custom_call" | custom-call | flops 2304000000 | tf_op jit(solution)/shard_map/pallas_call | solution.py:111
  81.0 3.6 %collective-permute-start.20 = (bf16[96,3072]{1,0:T(8,128)(2,1)S(1)}, bf16[96,3072]{1,0:T(8,128)(2,1)S(1)}, u32[]{:S(2)}, u32[]{:S(2)}) collective-permute-start(bf16[96,3072]{1,0:T(8,128)(2,1)S(1)} %shard_map.67), channel_id=1, source_target_pairs={{0,2},{1,3},{2,0},{3,1},{4,6},{5,7},{6,4},{7,5},{8,10},{9,11},{10,... | collective-permute-start | bytes 1769480 | tf_op jit(solution)/shard_map/ppermute | solution.py:23
  84.6 7.4 %collective-permute-done.16.refs_3_ = bf16[96,3072]{1,0:T(8,128)(2,1)S(1)} collective-permute-done((bf16[96,3072]{1,0:T(8,128)(2,1)S(1)}, bf16[96,3072]{1,0:T(8,128)(2,1)S(1)}, u32[]{:S(2)}, u32[]{:S(2)}) %collective-permute-start.16) | collective-permute-done | bytes 589856 | tf_op jit(solution)/shard_map/ppermute | solution.py:23
  92.0 0.1 add_convert_fusion.2
  92.2 0.1 add_convert_fusion.11
  92.3 0.7 collective-permute-start.13
  93.0 3.8 %shard_map.68 = bf16[96,3072]{1,0:T(8,128)(2,1)S(1)} custom-call(s32[3]{0:T(128)S(1)} %get-tuple-element.61.refs_0_, s32[1,768]{1,0:T(1,128)S(1)} %dynamic-slice_bitcast_fusion.3.refs_1_, f32[1,768]{1,0:T(1,128)S(1)} %dynamic-slice_bitcast_fusion.2.refs_2_, bf16[96,3072]{1,0:T(8,128)(2,1)S(1)} %collective-permute-done.16.refs_3_, ...), custom_call_target="tpu_custom_call" | custom-call | flops 2304000000 | tf_op jit(solution)/shard_map/pallas_call | solution.py:111
  96.8 3.4 %collective-permute-start.24 = (bf16[96,3072]{1,0:T(8,128)(2,1)S(1)}, bf16[96,3072]{1,0:T(8,128)(2,1)S(1)}, u32[]{:S(2)}, u32[]{:S(2)}) collective-permute-start(bf16[96,3072]{1,0:T(8,128)(2,1)S(1)} %shard_map.68), channel_id=1, source_target_pairs={{0,2},{1,3},{2,0},{3,1},{4,6},{5,7},{6,4},{7,5},{8,10},{9,11},{10,... | collective-permute-start | bytes 1769480 | tf_op jit(solution)/shard_map/ppermute | solution.py:23
  100.2 4.4 %collective-permute-done.20 = bf16[96,3072]{1,0:T(8,128)(2,1)S(1)} collective-permute-done((bf16[96,3072]{1,0:T(8,128)(2,1)S(1)}, bf16[96,3072]{1,0:T(8,128)(2,1)S(1)}, u32[]{:S(2)}, u32[]{:S(2)}) %collective-permute-start.20) | collective-permute-done | bytes 589856 | tf_op jit(solution)/shard_map/ppermute | solution.py:23
  104.6 0.2 add_convert_fusion.1
  104.8 0.1 collective-permute-start.21
  104.9 0.1 add_convert_fusion.9
  105.0 2.3 %collective-permute-start.18 = (bf16[48,3072]{1,0:T(8,128)(2,1)S(1)}, bf16[48,3072]{1,0:T(8,128)(2,1)S(1)}, u32[]{:S(2)}, u32[]{:S(2)}) collective-permute-start(bf16[48,3072]{1,0:T(8,128)(2,1)S(1)} %add_convert_fusion.9), channel_id=1, source_target_pairs={{0,2},{1,3},{2,0},{3,1},{4,6},{5,7},{6,4},{7,5},{8,10},{9,11},{10,... | collective-permute-start | bytes 884744 | tf_op jit(solution)/shard_map/ppermute | solution.py:23
  107.3 15.6 %collective-permute-done.24 = bf16[96,3072]{1,0:T(8,128)(2,1)S(1)} collective-permute-done((bf16[96,3072]{1,0:T(8,128)(2,1)S(1)}, bf16[96,3072]{1,0:T(8,128)(2,1)S(1)}, u32[]{:S(2)}, u32[]{:S(2)}) %collective-permute-start.24) | collective-permute-done | bytes 589856 | tf_op jit(solution)/shard_map/ppermute | solution.py:23
  122.8 0.2 add_convert_fusion
  123.2 0.1 add_convert_fusion.7
  123.2 2.1 %collective-permute-start.22 = (bf16[48,3072]{1,0:T(8,128)(2,1)S(1)}, bf16[48,3072]{1,0:T(8,128)(2,1)S(1)}, u32[]{:S(2)}, u32[]{:S(2)}) collective-permute-start(bf16[48,3072]{1,0:T(8,128)(2,1)S(1)} %add_convert_fusion.7), channel_id=1, source_target_pairs={{0,2},{1,3},{2,0},{3,1},{4,6},{5,7},{6,4},{7,5},{8,10},{9,11},{10,... | collective-permute-start | bytes 884744 | tf_op jit(solution)/shard_map/ppermute | solution.py:23
  125.3 0.7 collective-permute-done.18
  126.0 0.3 add_convert_fusion.8
  126.4 1.5 collective-permute-start.14
  128.0 0.1 add_convert_fusion.5
  128.0 6.0 %collective-permute-done.14 = bf16[48,3072]{1,0:T(8,128)(2,1)S(1)} collective-permute-done((bf16[48,3072]{1,0:T(8,128)(2,1)S(1)}, bf16[48,3072]{1,0:T(8,128)(2,1)S(1)}, u32[]{:S(2)}, u32[]{:S(2)}) %collective-permute-start.14) | collective-permute-done | bytes 294944 | tf_op jit(solution)/shard_map/ppermute | solution.py:45
  134.0 1.7 %collective-permute-start.26 = (bf16[48,3072]{1,0:T(8,128)(2,1)S(1)}, bf16[48,3072]{1,0:T(8,128)(2,1)S(1)}, u32[]{:S(2)}, u32[]{:S(2)}) collective-permute-start(bf16[48,3072]{1,0:T(8,128)(2,1)S(1)} %add_convert_fusion.5), channel_id=1, source_target_pairs={{0,2},{1,3},{2,0},{3,1},{4,6},{5,7},{6,4},{7,5},{8,10},{9,11},{10,... | collective-permute-start | bytes 884744 | tf_op jit(solution)/shard_map/ppermute | solution.py:23
  135.8 0.6 collective-permute-start.19
  136.4 4.7 %collective-permute-done.26 = bf16[48,3072]{1,0:T(8,128)(2,1)S(1)} collective-permute-done((bf16[48,3072]{1,0:T(8,128)(2,1)S(1)}, bf16[48,3072]{1,0:T(8,128)(2,1)S(1)}, u32[]{:S(2)}, u32[]{:S(2)}) %collective-permute-start.26) | collective-permute-done | bytes 294944 | tf_op jit(solution)/shard_map/ppermute | solution.py:23
  141.1 1.4 add_convert_fusion.6
  142.5 1.0 collective-permute-done.19
  143.5 2.7 %collective-permute-start.23 = (bf16[48,3072]{1,0:T(8,128)(2,1)S(1)}, bf16[48,3072]{1,0:T(8,128)(2,1)S(1)}, u32[]{:S(2)}, u32[]{:S(2)}) collective-permute-start(bf16[48,3072]{1,0:T(8,128)(2,1)S(1)} %get-tuple-element.78), channel_id=1, source_target_pairs={{0,9},{1,8},{2,11},{3,10},{4,13},{5,12},{6,15},{7,14},{8,17},{9,16... | collective-permute-start | bytes 884744 | tf_op jit(solution)/shard_map/ppermute | solution.py:45
  146.2 7.5 %collective-permute-done.27 = bf16[48,3072]{1,0:T(8,128)(2,1)S(1)} collective-permute-done((bf16[48,3072]{1,0:T(8,128)(2,1)S(1)}, bf16[48,3072]{1,0:T(8,128)(2,1)S(1)}, u32[]{:S(2)}, u32[]{:S(2)}) %collective-permute-start.27) | collective-permute-done | bytes 294944 | tf_op jit(solution)/shard_map/ppermute | solution.py:45
  153.7 4.6 %collective-permute-done.23 = bf16[48,3072]{1,0:T(8,128)(2,1)S(1)} collective-permute-done((bf16[48,3072]{1,0:T(8,128)(2,1)S(1)}, bf16[48,3072]{1,0:T(8,128)(2,1)S(1)}, u32[]{:S(2)}, u32[]{:S(2)}) %collective-permute-start.23) | collective-permute-done | bytes 294944 | tf_op jit(solution)/shard_map/ppermute | solution.py:45
  158.3 0.2 broadcast_select_fusion.7
  158.5 1.1 maximum_bitcast_fusion
  (43 shorter events, 0.6 us)
Async XLA Ops:
  0.0 7.2 %copy-start = (f32[1,2,6,128]{3,1,2,0:T(2,128)S(1)}, f32[1,2,6,128]{3,1,2,0:T(2,128)}, u32[]{:S(2)}) copy-start(f32[1,2,6,128]{3,1,2,0:T(2,128)} %param.11) | copy-start | bytes 18436
  0.0 7.2 %copy-start.1 = (bf16[1,3072,512]{2,1,0:T(8,128)(2,1)S(1)}, bf16[1,3072,512]{2,1,0:T(8,128)(2,1)}, u32[]{:S(2)}) copy-start(bf16[1,3072,512]{2,1,0:T(8,128)(2,1)} %param.7) | copy-start | bytes 9437188
  2.3 0.8 copy-start.4
  2.3 4.9 %copy-start.6 = (s32[1,2,6,128]{3,1,2,0:T(2,128)S(1)}, s32[1,2,6,128]{3,1,2,0:T(2,128)}, u32[]{:S(2)}) copy-start(s32[1,2,6,128]{3,1,2,0:T(2,128)} %param.10) | copy-start | bytes 18436
  2.3 4.9 %collective-permute-start = (bf16[96,3072]{1,0:T(8,128)(2,1)}, bf16[96,3072]{1,0:T(8,128)(2,1)}, u32[]{:S(2)}, u32[]{:S(2)}) collective-permute-start(bf16[96,3072]{1,0:T(8,128)(2,1)} %get-tuple-element.74), channel_id=1, source_target_pairs={{0,1},{1,0},{2,3},{3,2},{4,5},{5,4},{6,7},{7,6},{8,9},{9,8},{10,11... | collective-permute-start | bytes 1769480 | tf_op jit(solution)/shard_map/ppermute | solution.py:34
  3.9 11.2 %collective-permute-start.1 = (bf16[48,3072]{1,0:T(8,128)(2,1)}, bf16[48,3072]{1,0:T(8,128)(2,1)}, u32[]{:S(2)}, u32[]{:S(2)}) collective-permute-start(bf16[48,3072]{1,0:T(8,128)(2,1)} %get-tuple-element.46.refs_3_), channel_id=1, source_target_pairs={{0,2},{1,3},{2,0},{3,1},{4,6},{5,7},{6,4},{7,5},{8,10},{9,11},{10,... | collective-permute-start | bytes 884744 | tf_op jit(solution)/shard_map/ppermute | solution.py:23
  7.2 39.1 %collective-permute-start.4 = (bf16[3072,512]{1,0:T(8,128)(2,1)S(1)}, bf16[3072,512]{1,0:T(8,128)(2,1)S(1)}, u32[]{:S(2)}, u32[]{:S(2)}) collective-permute-start(bf16[3072,512]{1,0:T(8,128)(2,1)S(1)} %bitcast.34), channel_id=1, source_target_pairs={{0,1},{1,0},{2,3},{3,2},{4,5},{5,4},{6,7},{7,6},{8,9},{9,8},{10,11... | collective-permute-start | bytes 9437192 | tf_op jit(solution)/shard_map/ppermute | solution.py:34
  7.3 43.6 %collective-permute-start.5 = (bf16[3072,512]{1,0:T(8,128)(2,1)}, bf16[3072,512]{1,0:T(8,128)(2,1)S(1)}, u32[]{:S(2)}, u32[]{:S(2)}) collective-permute-start(bf16[3072,512]{1,0:T(8,128)(2,1)} %bitcast.40), channel_id=1, source_target_pairs={{0,1},{1,0},{2,3},{3,2},{4,5},{5,4},{6,7},{7,6},{8,9},{9,8},{10,11... | collective-permute-start | bytes 9437192 | tf_op jit(solution)/shard_map/ppermute | solution.py:34
  7.8 43.1 %collective-permute-start.6 = (bf16[512,3072]{1,0:T(8,128)(2,1)}, bf16[512,3072]{1,0:T(8,128)(2,1)S(1)}, u32[]{:S(2)}, u32[]{:S(2)}) collective-permute-start(bf16[512,3072]{1,0:T(8,128)(2,1)} %bitcast.46), channel_id=1, source_target_pairs={{0,1},{1,0},{2,3},{3,2},{4,5},{5,4},{6,7},{7,6},{8,9},{9,8},{10,11... | collective-permute-start | bytes 9437192 | tf_op jit(solution)/shard_map/ppermute | solution.py:34
  9.0 24.9 %collective-permute-start.7 = (bf16[144,3072]{1,0:T(8,128)(2,1)S(1)}, bf16[144,3072]{1,0:T(8,128)(2,1)S(1)}, u32[]{:S(2)}, u32[]{:S(2)}) collective-permute-start(bf16[144,3072]{1,0:T(8,128)(2,1)S(1)} %pad_maximum_fusion), channel_id=1, source_target_pairs={{0,2},{1,3},{2,0},{3,1},{4,6},{5,7},{6,4},{7,5},{8,10},{9,11},{10,... | collective-permute-start | bytes 2654216 | tf_op jit(solution)/shard_map/ppermute | solution.py:23
  16.2 3.0 %collective-permute-start.2 = (bf16[96,3072]{1,0:T(8,128)(2,1)S(1)}, bf16[96,3072]{1,0:T(8,128)(2,1)S(1)}, u32[]{:S(2)}, u32[]{:S(2)}) collective-permute-start(bf16[96,3072]{1,0:T(8,128)(2,1)S(1)} %pad_maximum_fusion.1), channel_id=1, source_target_pairs={{2,4},{3,5},{4,2},{5,3},{0,1},{1,0},{6,7},{7,6},{10,12},{11,13},{1... | collective-permute-start | bytes 1769480 | tf_op jit(solution)/shard_map/ppermute | solution.py:29
  16.2 34.7 %copy-start.3 = (bf16[1,512,3072]{2,1,0:T(8,128)(2,1)S(1)}, bf16[1,512,3072]{2,1,0:T(8,128)(2,1)}, u32[]{:S(2)}) copy-start(bf16[1,512,3072]{2,1,0:T(8,128)(2,1)} %param.9) | copy-start | bytes 9437188
  19.1 26.6 %collective-permute-start.3 = (bf16[96,3072]{1,0:T(8,128)(2,1)S(1)}, bf16[96,3072]{1,0:T(8,128)(2,1)S(1)}, u32[]{:S(2)}, u32[]{:S(2)}) collective-permute-start(bf16[96,3072]{1,0:T(8,128)(2,1)S(1)} %collective-permute-done.2.refs_4_), channel_id=1, source_target_pairs={{0,2},{1,3},{2,0},{3,1},{4,6},{5,7},{6,4},{7,5},{8,10},{9,11},{10,... | collective-permute-start | bytes 1769480 | tf_op jit(solution)/shard_map/ppermute | solution.py:23
  34.0 17.0 %copy-start.2 = (bf16[1,3072,512]{2,1,0:T(8,128)(2,1)S(1)}, bf16[1,3072,512]{2,1,0:T(8,128)(2,1)}, u32[]{:S(2)}) copy-start(bf16[1,3072,512]{2,1,0:T(8,128)(2,1)} %param.8) | copy-start | bytes 9437188
  34.0 11.7 %collective-permute-start.10 = (bf16[96,3072]{1,0:T(8,128)(2,1)S(1)}, bf16[96,3072]{1,0:T(8,128)(2,1)S(1)}, u32[]{:S(2)}, u32[]{:S(2)}) collective-permute-start(bf16[96,3072]{1,0:T(8,128)(2,1)S(1)} %pad_maximum_fusion.3), channel_id=1, source_target_pairs={{2,4},{3,5},{4,2},{5,3},{0,1},{1,0},{6,7},{7,6},{10,12},{11,13},{1... | collective-permute-start | bytes 1769480 | tf_op jit(solution)/shard_map/ppermute | solution.py:29
  45.7 9.1 %collective-permute-start.8 = (bf16[96,3072]{1,0:T(8,128)(2,1)S(1)}, bf16[96,3072]{1,0:T(8,128)(2,1)S(1)}, u32[]{:S(2)}, u32[]{:S(2)}) collective-permute-start(bf16[96,3072]{1,0:T(8,128)(2,1)S(1)} %pad_maximum_fusion.2), channel_id=1, source_target_pairs={{2,4},{3,5},{4,2},{5,3},{0,1},{1,0},{6,7},{7,6},{10,12},{11,13},{1... | collective-permute-start | bytes 1769480 | tf_op jit(solution)/shard_map/ppermute | solution.py:29
  45.8 30.9 %collective-permute-start.15 = (bf16[96,3072]{1,0:T(8,128)(2,1)S(1)}, bf16[96,3072]{1,0:T(8,128)(2,1)S(1)}, u32[]{:S(2)}, u32[]{:S(2)}) collective-permute-start(bf16[96,3072]{1,0:T(8,128)(2,1)S(1)} %pad_maximum_fusion.4), channel_id=1, source_target_pairs={{2,4},{3,5},{4,2},{5,3},{0,1},{1,0},{6,7},{7,6},{10,12},{11,13},{1... | collective-permute-start | bytes 1769480 | tf_op jit(solution)/shard_map/ppermute | solution.py:29
  46.4 26.3 %collective-permute-start.11 = (bf16[96,3072]{1,0:T(8,128)(2,1)S(1)}, bf16[96,3072]{1,0:T(8,128)(2,1)S(1)}, u32[]{:S(2)}, u32[]{:S(2)}) collective-permute-start(bf16[96,3072]{1,0:T(8,128)(2,1)S(1)} %collective-permute-done.10.refs_4_), channel_id=1, source_target_pairs={{0,2},{1,3},{2,0},{3,1},{4,6},{5,7},{6,4},{7,5},{8,10},{9,11},{10,... | collective-permute-start | bytes 1769480 | tf_op jit(solution)/shard_map/ppermute | solution.py:23
  54.9 22.0 %collective-permute-start.9 = (bf16[96,3072]{1,0:T(8,128)(2,1)S(1)}, bf16[96,3072]{1,0:T(8,128)(2,1)S(1)}, u32[]{:S(2)}, u32[]{:S(2)}) collective-permute-start(bf16[96,3072]{1,0:T(8,128)(2,1)S(1)} %broadcast_select_fusion.5), channel_id=1, source_target_pairs={{0,2},{1,3},{2,0},{3,1},{4,6},{5,7},{6,4},{7,5},{8,10},{9,11},{10,... | collective-permute-start | bytes 1769480 | tf_op jit(solution)/shard_map/ppermute | solution.py:23
  76.8 15.2 %collective-permute-start.16 = (bf16[96,3072]{1,0:T(8,128)(2,1)S(1)}, bf16[96,3072]{1,0:T(8,128)(2,1)S(1)}, u32[]{:S(2)}, u32[]{:S(2)}) collective-permute-start(bf16[96,3072]{1,0:T(8,128)(2,1)S(1)} %broadcast_select_fusion.3), channel_id=1, source_target_pairs={{0,2},{1,3},{2,0},{3,1},{4,6},{5,7},{6,4},{7,5},{8,10},{9,11},{10,... | collective-permute-start | bytes 1769480 | tf_op jit(solution)/shard_map/ppermute | solution.py:23
  77.0 15.1 %collective-permute-start.12 = (bf16[96,3072]{1,0:T(8,128)(2,1)S(1)}, bf16[96,3072]{1,0:T(8,128)(2,1)S(1)}, u32[]{:S(2)}, u32[]{:S(2)}) collective-permute-start(bf16[96,3072]{1,0:T(8,128)(2,1)S(1)} %add_convert_fusion.3), channel_id=1, source_target_pairs={{2,4},{3,5},{4,2},{5,3},{0,1},{1,0},{6,7},{7,6},{10,12},{11,13},{1... | collective-permute-start | bytes 1769480 | tf_op jit(solution)/shard_map/ppermute | solution.py:29
  81.0 23.7 %collective-permute-start.20 = (bf16[96,3072]{1,0:T(8,128)(2,1)S(1)}, bf16[96,3072]{1,0:T(8,128)(2,1)S(1)}, u32[]{:S(2)}, u32[]{:S(2)}) collective-permute-start(bf16[96,3072]{1,0:T(8,128)(2,1)S(1)} %shard_map.67), channel_id=1, source_target_pairs={{0,2},{1,3},{2,0},{3,1},{4,6},{5,7},{6,4},{7,5},{8,10},{9,11},{10,... | collective-permute-start | bytes 1769480 | tf_op jit(solution)/shard_map/ppermute | solution.py:23
  92.3 33.0 %collective-permute-start.13 = (bf16[48,3072]{1,0:T(8,128)(2,1)S(1)}, bf16[48,3072]{1,0:T(8,128)(2,1)S(1)}, u32[]{:S(2)}, u32[]{:S(2)}) collective-permute-start(bf16[48,3072]{1,0:T(8,128)(2,1)S(1)} %add_convert_fusion.11), channel_id=1, source_target_pairs={{0,2},{1,3},{2,0},{3,1},{4,6},{5,7},{6,4},{7,5},{8,10},{9,11},{10,... | collective-permute-start | bytes 884744 | tf_op jit(solution)/shard_map/ppermute | solution.py:23
  93.0 11.9 %collective-permute-start.17 = (bf16[96,3072]{1,0:T(8,128)(2,1)S(1)}, bf16[96,3072]{1,0:T(8,128)(2,1)S(1)}, u32[]{:S(2)}, u32[]{:S(2)}) collective-permute-start(bf16[96,3072]{1,0:T(8,128)(2,1)S(1)} %add_convert_fusion.2), channel_id=1, source_target_pairs={{2,4},{3,5},{4,2},{5,3},{0,1},{1,0},{6,7},{7,6},{10,12},{11,13},{1... | collective-permute-start | bytes 1769480 | tf_op jit(solution)/shard_map/ppermute | solution.py:29
  96.8 26.0 %collective-permute-start.24 = (bf16[96,3072]{1,0:T(8,128)(2,1)S(1)}, bf16[96,3072]{1,0:T(8,128)(2,1)S(1)}, u32[]{:S(2)}, u32[]{:S(2)}) collective-permute-start(bf16[96,3072]{1,0:T(8,128)(2,1)S(1)} %shard_map.68), channel_id=1, source_target_pairs={{0,2},{1,3},{2,0},{3,1},{4,6},{5,7},{6,4},{7,5},{8,10},{9,11},{10,... | collective-permute-start | bytes 1769480 | tf_op jit(solution)/shard_map/ppermute | solution.py:23
  104.8 18.3 %collective-permute-start.21 = (bf16[96,3072]{1,0:T(8,128)(2,1)S(1)}, bf16[96,3072]{1,0:T(8,128)(2,1)S(1)}, u32[]{:S(2)}, u32[]{:S(2)}) collective-permute-start(bf16[96,3072]{1,0:T(8,128)(2,1)S(1)} %add_convert_fusion.1), channel_id=1, source_target_pairs={{2,4},{3,5},{4,2},{5,3},{0,1},{1,0},{6,7},{7,6},{10,12},{11,13},{1... | collective-permute-start | bytes 1769480 | tf_op jit(solution)/shard_map/ppermute | solution.py:29
  105.0 21.0 %collective-permute-start.18 = (bf16[48,3072]{1,0:T(8,128)(2,1)S(1)}, bf16[48,3072]{1,0:T(8,128)(2,1)S(1)}, u32[]{:S(2)}, u32[]{:S(2)}) collective-permute-start(bf16[48,3072]{1,0:T(8,128)(2,1)S(1)} %add_convert_fusion.9), channel_id=1, source_target_pairs={{0,2},{1,3},{2,0},{3,1},{4,6},{5,7},{6,4},{7,5},{8,10},{9,11},{10,... | collective-permute-start | bytes 884744 | tf_op jit(solution)/shard_map/ppermute | solution.py:23
  123.0 3.0 %copy-start.5 = (bf16[96,3072]{1,0:T(8,128)(2,1)S(1)}, bf16[96,3072]{1,0:T(8,128)(2,1)}, u32[]{:S(2)}) copy-start(bf16[96,3072]{1,0:T(8,128)(2,1)} %copy-done.4) | copy-start | bytes 1769476
  123.0 4.9 %collective-permute-start.25 = (bf16[96,3072]{1,0:T(8,128)(2,1)S(1)}, bf16[96,3072]{1,0:T(8,128)(2,1)S(1)}, u32[]{:S(2)}, u32[]{:S(2)}) collective-permute-start(bf16[96,3072]{1,0:T(8,128)(2,1)S(1)} %add_convert_fusion), channel_id=1, source_target_pairs={{2,4},{3,5},{4,2},{5,3},{0,1},{1,0},{6,7},{7,6},{10,12},{11,13},{1... | collective-permute-start | bytes 1769480 | tf_op jit(solution)/shard_map/ppermute | solution.py:29
  123.2 13.1 %collective-permute-start.22 = (bf16[48,3072]{1,0:T(8,128)(2,1)S(1)}, bf16[48,3072]{1,0:T(8,128)(2,1)S(1)}, u32[]{:S(2)}, u32[]{:S(2)}) collective-permute-start(bf16[48,3072]{1,0:T(8,128)(2,1)S(1)} %add_convert_fusion.7), channel_id=1, source_target_pairs={{0,2},{1,3},{2,0},{3,1},{4,6},{5,7},{6,4},{7,5},{8,10},{9,11},{10,... | collective-permute-start | bytes 884744 | tf_op jit(solution)/shard_map/ppermute | solution.py:23
  126.4 7.7 %collective-permute-start.14 = (bf16[48,3072]{1,0:T(8,128)(2,1)S(1)}, bf16[48,3072]{1,0:T(8,128)(2,1)S(1)}, u32[]{:S(2)}, u32[]{:S(2)}) collective-permute-start(bf16[48,3072]{1,0:T(8,128)(2,1)S(1)} %get-tuple-element.81), channel_id=1, source_target_pairs={{0,8},{1,9},{2,10},{3,11},{4,12},{5,13},{6,14},{7,15},{8,16},{9,17... | collective-permute-start | bytes 884744 | tf_op jit(solution)/shard_map/ppermute | solution.py:45
  134.0 7.0 %collective-permute-start.26 = (bf16[48,3072]{1,0:T(8,128)(2,1)S(1)}, bf16[48,3072]{1,0:T(8,128)(2,1)S(1)}, u32[]{:S(2)}, u32[]{:S(2)}) collective-permute-start(bf16[48,3072]{1,0:T(8,128)(2,1)S(1)} %add_convert_fusion.5), channel_id=1, source_target_pairs={{0,2},{1,3},{2,0},{3,1},{4,6},{5,7},{6,4},{7,5},{8,10},{9,11},{10,... | collective-permute-start | bytes 884744 | tf_op jit(solution)/shard_map/ppermute | solution.py:23
  135.8 7.7 %collective-permute-start.19 = (bf16[48,3072]{1,0:T(8,128)(2,1)S(1)}, bf16[48,3072]{1,0:T(8,128)(2,1)S(1)}, u32[]{:S(2)}, u32[]{:S(2)}) collective-permute-start(bf16[48,3072]{1,0:T(8,128)(2,1)S(1)} %get-tuple-element.80), channel_id=1, source_target_pairs={{0,8},{1,9},{2,10},{3,11},{4,12},{5,13},{6,14},{7,15},{8,16},{9,17... | collective-permute-start | bytes 884744 | tf_op jit(solution)/shard_map/ppermute | solution.py:45
  143.5 10.3 %collective-permute-start.27 = (bf16[48,3072]{1,0:T(8,128)(2,1)S(1)}, bf16[48,3072]{1,0:T(8,128)(2,1)S(1)}, u32[]{:S(2)}, u32[]{:S(2)}) collective-permute-start(bf16[48,3072]{1,0:T(8,128)(2,1)S(1)} %get-tuple-element.70), channel_id=1, source_target_pairs={{0,9},{1,8},{2,11},{3,10},{4,13},{5,12},{6,15},{7,14},{8,17},{9,16... | collective-permute-start | bytes 884744 | tf_op jit(solution)/shard_map/ppermute | solution.py:45
  143.5 14.9 %collective-permute-start.23 = (bf16[48,3072]{1,0:T(8,128)(2,1)S(1)}, bf16[48,3072]{1,0:T(8,128)(2,1)S(1)}, u32[]{:S(2)}, u32[]{:S(2)}) collective-permute-start(bf16[48,3072]{1,0:T(8,128)(2,1)S(1)} %get-tuple-element.78), channel_id=1, source_target_pairs={{0,9},{1,8},{2,11},{3,10},{4,13},{5,12},{6,15},{7,14},{8,17},{9,16... | collective-permute-start | bytes 884744 | tf_op jit(solution)/shard_map/ppermute | solution.py:45
